TPU v7x, 128 devices: a whole 4x4x4 slice. The times are simulated.
128 devices in a mesh: frame: 4 (over z), batch: 32 (over x, y, core).
Axes of the slice: x: 4, y: 4, z: 4, core: 2. Of those that a mesh axis runs over, the one named last changes fastest.
Arguments:
- frames: bfloat16 [32, 4, 1024, 256], P('batch', None, 'frame'), may hold values from -6 to 6
- utt_len: int32 [32, 4], P('batch'), may hold values from 103 to 1024, as said below
- token_ids: int32 [32, 4, 128], P('batch', 'frame'), may hold values from 0 to 4999
- tok_len: int32 [32, 4], P('batch', 'frame'), may hold values from 38 to 128, as said below
- step: int32 [1], replicated, may hold values from 12500 to 99999
- embed: bfloat16 [5000, 256], replicated, may hold values from -0.375 to 0.375
- norm_gain: float32 [5, 256], replicated, may hold values from 0.5 to 1.5
- norm_bias: float32 [5, 256], replicated, may hold values from -1.25 to 1.25
- attn_in: bfloat16 [3, 256, 768], replicated, may hold values from -0.375 to 0.375
- attn_in_bias: float32 [3, 512], replicated, may hold values from -1.25 to 1.25
- attn_out: bfloat16 [3, 256, 256], replicated, may hold values from -1.5 to 1.5
- attn_out_bias: float32 [3, 256], replicated, may hold values from -1.25 to 1.25
- ff_in: bfloat16 [2, 256, 2048], replicated, may hold values from -0.375 to 0.375
- ff_in_bias: float32 [2, 2048], replicated, may hold values from -1.25 to 1.25
- ff_out: bfloat16 [2, 2048, 256], replicated, may hold values from -0.125 to 0.125
- ff_out_bias: float32 [2, 256], replicated, may hold values from -1.25 to 1.25
- cotangent: bfloat16 [32, 4, 128, 256], P('batch', 'frame'), may hold values from -6 to 6
Outputs:
- dec_out: bfloat16 [32, 4, 128, 256], P('batch', 'frame')
- frames_grad: float32 [32, 4, 1024, 256], P('batch', None, 'frame')
- embed_grad: float32 [5000, 256], replicated
- norm_gain_grad: float32 [5, 256], replicated
- norm_bias_grad: float32 [5, 256], replicated
- attn_in_grad: float32 [3, 256, 768], replicated
- attn_in_bias_grad: float32 [3, 512], replicated
- attn_out_grad: float32 [3, 256, 256], replicated
- attn_out_bias_grad: float32 [3, 256], replicated
- ff_in_grad: float32 [2, 256, 2048], replicated
- ff_in_bias_grad: float32 [2, 2048], replicated
- ff_out_grad: float32 [2, 2048, 256], replicated
- ff_out_bias_grad: float32 [2, 256], replicated
Inputs may be any that keep to these rules, and one draw needn't show every extreme that they name: `utt_len`: in every group one utterance, drawn from the seed, has exactly 1024 frames. `tok_len`: in every group one transcript, drawn from the seed, has exactly 128 tokens.
All inputs are finite; a program needn't handle non-finite values.
Results may differ from a plain program's by a relative error of at most 0.018.
Values may be sent and summed in bfloat16 or wider, within the bound.
No kernel may reach another device: no remote copies, remote signals or barrier semaphores. Data moves between devices by JAX's collectives and lax.ppermute only.
A program may use at most 192 MiB of HBM per device.

v0:
```python
import functools
import math

import jax
import jax.numpy as jnp
from jax import lax
from jax.experimental import pallas as pl
from jax.experimental.pallas import tpu as pltpu
from jax.sharding import Mesh, PartitionSpec as P

HEADS = 4
HEAD_DIM = 64
WARMUP = 25000
EPSILON = 1e-05
MASKED = -1e30
BF = jnp.bfloat16
F32 = jnp.float32
GELU_A = math.sqrt(2.0 / math.pi)
GELU_B = GELU_A * 0.044715
SMALL = 32
FEED_CHUNK = 1024
SPILL = 64


def nn(left, right):
    return lax.dot_general(left, right, (((1,), (0,)), ((), ())), preferred_element_type=F32)


def nt(left, right):
    return lax.dot_general(left, right, (((1,), (1,)), ((), ())), preferred_element_type=F32)


def hand_out(sems, *pairs):
    copies = [pltpu.make_async_copy(held, ref, sems.at[i]) for i, (held, ref) in enumerate(pairs)]
    for copy in copies:
        copy.start()
    for copy in copies:
        copy.wait()


def normalise(states):
    average = jnp.mean(states, axis=-1, keepdims=True)
    centred = states - average
    scale = lax.rsqrt(jnp.mean(centred * centred, axis=-1, keepdims=True) + EPSILON)
    return centred * scale, scale


def norm_backward(grad, unit, scale, gain):
    grad_unit = grad * gain
    mean_grad = jnp.mean(grad_unit, axis=-1, keepdims=True)
    mean_along = jnp.mean(grad_unit * unit, axis=-1, keepdims=True)
    grad_states = scale * (grad_unit - mean_grad - unit * mean_along)
    return grad_states, col_sum(grad * unit), col_sum(grad)


def col_sum(matrix):
    return jnp.sum(matrix.astype(F32), axis=0, keepdims=True)


def gelu_value(hidden):
    inner = hidden * (GELU_A + GELU_B * (hidden * hidden))
    return hidden * (0.5 + 0.5 * jnp.tanh(inner))


def gelu_both(hidden):
    square = hidden * hidden
    bent = jnp.tanh(hidden * (GELU_A + GELU_B * square))
    half = 0.5 + 0.5 * bent
    slope = half + (0.5 * hidden) * (1.0 - bent * bent) * (GELU_A + 3.0 * GELU_B * square)
    return hidden * half, slope


def lanes_of(head):
    return slice(128 * (head // 2), 128 * (head // 2) + 128)


def rows_of(head):
    return slice(HEAD_DIM * head, HEAD_DIM * head + HEAD_DIM)


def each_pair(step):
    def body(pair, carry):
        step(pl.multiple_of(pair * 2 * HEAD_DIM, 2 * HEAD_DIM), pair)
        return carry

    lax.fori_loop(0, HEADS // 2, body, 0)


def head_rows(at, odd):
    return pl.ds(pl.multiple_of(at + HEAD_DIM * odd, HEAD_DIM), HEAD_DIM)


def own_lanes(pair, head):
    lane = lax.broadcasted_iota(jnp.int32, pair.shape, 1)
    mine = (lane < HEAD_DIM) if head % 2 == 0 else (lane >= HEAD_DIM)
    return jnp.where(mine, pair, jnp.zeros_like(pair))


def spare_lane(head):
    return HEAD_DIM if head % 2 == 0 else 0


def with_one(query, head):
    lane = lax.broadcasted_iota(jnp.int32, query.shape, 1)
    return jnp.where(lane == spare_lane(head), jnp.ones_like(query), query)


def with_mask(key_pair, head, length):
    lane = lax.broadcasted_iota(jnp.int32, key_pair.shape, 1)
    row = lax.broadcasted_iota(jnp.int32, key_pair.shape, 0)
    bias = jnp.where(row < length, 0.0, MASKED).astype(BF)
    return jnp.where(lane == spare_lane(head), bias, key_pair)


def part_spec(shape, layers, at):
    index = (at,) + (0,) * (len(shape) - 1)
    return pl.BlockSpec((layers,) + shape[1:], lambda *g: index, pipeline_mode=pl.Buffered(1))


def call(kernel, outs, args, scalars=(), scratch=(), flops=0, aliases=None, limit=61):
    in_specs = []
    for a in args:
        if not isinstance(a, tuple):
            in_specs.append(part_spec(a.shape, a.shape[0], 0))
        elif a[1] is None or a[1] == "vmem":
            in_specs.append(pl.BlockSpec(memory_space=pl.ANY))
        else:
            in_specs.append(part_spec(a[0].shape, None, a[1]))
    spaces = {None: pltpu.HBM, "vmem": pltpu.VMEM}
    args = [a if isinstance(a, tuple) else (a, 0) for a in args]
    args = [a[0] if isinstance(a[1], int) else pltpu.with_memory_space_constraint(a[0], spaces[a[1]]) for a in args]
    out_specs = []
    for out in outs:
        if out[-1] is None:
            out_specs.append(pl.BlockSpec(memory_space=pltpu.HBM))
        elif isinstance(out[-1], int):
            out_specs.append(part_spec(out[0], out[2], out[3]))
        else:
            out_specs.append(part_spec(out[0], out[0][0], 0))
    size = sum(a.size * a.dtype.itemsize for a in args)
    size += sum(math.prod(out[0]) * jnp.dtype(out[1]).itemsize for out in outs)
    return pl.pallas_call(
        kernel,
        grid_spec=pltpu.PrefetchScalarGridSpec(
            num_scalar_prefetch=len(scalars),
            grid=(1,),
            in_specs=in_specs,
            out_specs=out_specs,
            scratch_shapes=list(scratch),
        ),
        out_shape=[
            (pltpu.HBM if out[-1] is None else jax.ShapeDtypeStruct)(out[0], out[1]) for out in outs
        ],
        input_output_aliases=aliases or {},
        compiler_params=pltpu.CompilerParams(vmem_limit_bytes=limit * 1024 * 1024),
        cost_estimate=pl.CostEstimate(flops=flops, bytes_accessed=size, transcendentals=0),
        name=kernel.__name__,
    )(*scalars, *args)


def decoder_start(
    tok_ref, emb_ref, gain_ref, shift_ref, in_ref, in_b_ref, out_ref, out_b_ref, cross_ref,
    y1_ref, norm_c_ref, qkv_ref, ctx_t_ref, prob_ref, norm_d_ref, cross_q_ref,
):
    text = emb_ref.shape[0]
    width = emb_ref.shape[1]
    start = emb_ref[...].astype(F32) * math.sqrt(width)
    unit, _ = normalise(start)
    norm_c = (unit * gain_ref[2:3] + shift_ref[2:3]).astype(BF)
    norm_c_ref[...] = norm_c
    flat = nn(norm_c, in_ref[...])
    query = (flat[:, :width] + in_b_ref[1:2, :width]).astype(BF)
    key = flat[:, width : 2 * width].astype(BF)
    value = (flat[:, 2 * width :] + in_b_ref[1:2, width:]).astype(BF)
    qkv_ref[:, :width] = query
    qkv_ref[:, width : 2 * width] = key
    qkv_ref[:, 2 * width :] = value
    value_t = value.astype(F32).T.astype(BF)
    key_at = lax.broadcasted_iota(jnp.int32, (text, text), 0)
    query_at = lax.broadcasted_iota(jnp.int32, (text, text), 1)
    seen = jnp.logical_and(key_at <= query_at, key_at < tok_ref[0])
    scaled = query * jnp.asarray(HEAD_DIM**-0.5, BF)
    parts = []
    for head in range(HEADS):
        lanes = lanes_of(head)
        score = nt(key[:, lanes], own_lanes(scaled[:, lanes], head))
        score = jnp.where(seen, score, MASKED)
        weight = jnp.exp(score - jnp.max(score, axis=0, keepdims=True))
        prob = weight / jnp.sum(weight, axis=0, keepdims=True)
        prob_ref[head] = prob
        parts.append(nn(value_t[rows_of(head)], prob.astype(BF)))
    ctx_t = jnp.concatenate(parts, axis=0)
    ctx_t_ref[...] = ctx_t.astype(BF)
    y1 = start + nn(ctx_t.T.astype(BF), out_ref[...]) + out_b_ref[1:2]
    y1_ref[...] = y1
    unit, _ = normalise(y1)
    norm_d = (unit * gain_ref[3:4] + shift_ref[3:4]).astype(BF)
    norm_d_ref[...] = norm_d
    cross_q_ref[...] = (nn(norm_d, cross_ref[:, :width]) + in_b_ref[2:3, :width]).astype(BF)


def encoder_forward(
    len_ref, at_ref, x_ref, gain_ref, shift_ref, in_ref, in_b_ref, out_ref, out_b_ref,
    w1_ref, b1_ref, w2_ref, b2_ref, cin_ref,
    qkv_ref, ctx_t_ref, lse_ref, h1_ref, mem_ref, cross_ref,
    value_t, act, between,
):
    rows, width = x_ref.shape
    unit, _ = normalise(x_ref[...].astype(F32))
    norm_a = (unit * gain_ref[0:1] + shift_ref[0:1]).astype(BF)
    qkv_ref[:, :width] = (nn(norm_a, in_ref[:, :width]) + in_b_ref[0:1, :width]).astype(BF)
    key = nn(norm_a, in_ref[:, width : 2 * width]).astype(BF)
    qkv_ref[:, width : 2 * width] = key
    value = (nn(norm_a, in_ref[:, 2 * width :]) + in_b_ref[0:1, width:]).astype(BF)
    qkv_ref[:, 2 * width :] = value
    value_t[...] = value.astype(F32).T.astype(BF)

    def attend(at, pair):
        keys = qkv_ref[:, pl.ds(width + at, 128)]
        queries = qkv_ref[:, pl.ds(at, 128)] * jnp.asarray(HEAD_DIM**-0.5, BF)
        for odd in range(2):
            query = with_one(own_lanes(queries, odd), odd)
            score = nt(with_mask(keys, odd, len_ref[at_ref[0]]), query)
            highest = jnp.max(score, axis=0, keepdims=True)
            weight = jnp.exp(score - highest)
            total = jnp.sum(weight, axis=0, keepdims=True)
            context = nn(value_t[head_rows(at, odd)], weight.astype(BF)) * (1.0 / total)
            ctx_t_ref[head_rows(at, odd)] = context.astype(BF)
            lse_ref[pl.ds(2 * pair + odd, 1)] = highest + jnp.log(total)

    each_pair(attend)
    context = ctx_t_ref[...].astype(F32).T.astype(BF)
    h1 = x_ref[...].astype(F32) + nn(context, out_ref[...]) + out_b_ref[0:1]
    h1_ref[...] = h1
    between()
    unit, _ = normalise(h1)
    norm_b = (unit * gain_ref[1:2] + shift_ref[1:2]).astype(BF)

    hidden = nn(norm_b, w1_ref[...]) + b1_ref[0:1]
    act[...] = gelu_value(hidden).astype(BF)
    memory = (h1_ref[...] + nn(act[...], w2_ref[...]) + b2_ref[0:1]).astype(BF)
    mem_ref[...] = memory
    cross_ref[:, :width] = nn(memory, cin_ref[:, width : 2 * width]).astype(BF)
    cross_ref[:, width:] = (nn(memory, cin_ref[:, 2 * width :]) + in_b_ref[2:3, width:]).astype(BF)


def decoder_main(
    tok_ref, len_ref, at_ref, core_ref,
    y1_ref, norm_d_ref, cross_q_ref, cross_ref, mem_ref, cot_ref, gain_ref, shift_ref,
    in2_ref, out2_ref, out_b_ref, w1_ref, b1_ref, w2_ref, b2_ref,
    dec_ref, dmem_ref, early_ref, grad_ref, small_ref,
    probs, turned, cross_t, dkv, dq_t,
):
    text, width = y1_ref.shape
    hidden_size = w1_ref.shape[1]
    slot = (core_ref[0], 1 - core_ref[0])
    small_ref[...] = jnp.zeros_like(small_ref)
    turned[...] = cross_ref[:, width:].astype(F32).T.astype(BF)

    def attend(at, pair):
        keys = cross_ref[:, pl.ds(at, 128)]
        queries = cross_q_ref[:, pl.ds(at, 128)] * jnp.asarray(HEAD_DIM**-0.5, BF)
        for odd in range(2):
            query = with_one(own_lanes(queries, odd), odd)
            score = nt(with_mask(keys, odd, len_ref[at_ref[0]]), query)
            weight = jnp.exp(score - jnp.max(score, axis=0, keepdims=True))
            prob = weight * (1.0 / jnp.sum(weight, axis=0, keepdims=True))
            probs[2 * pair + odd] = prob
            cross_t[head_rows(at, odd)] = nn(turned[head_rows(at, odd)], prob.astype(BF))

    each_pair(attend)
    context_t = cross_t[...]
    y2 = y1_ref[...] + nn(context_t.T.astype(BF), out2_ref[...]) + out_b_ref[2:3]
    unit_e, scale_e = normalise(y2)
    norm_e = (unit_e * gain_ref[4:5] + shift_ref[4:5]).astype(BF)
    norm_e_t = norm_e.astype(F32).T.astype(BF)
    valid = lax.broadcasted_iota(jnp.int32, (text, 1), 0) < tok_ref[0]
    grad_low = jnp.where(valid, cot_ref[...], jnp.zeros_like(cot_ref))
    grad = grad_low.astype(F32)
    grad_low_t = grad.T.astype(BF)
    chunk = 512

    def feed(index, sums):
        part = pl.ds(pl.multiple_of(index * chunk, chunk), chunk)
        hidden = nn(norm_e, w1_ref[:, part]) + b1_ref[1:2, part]
        value, slope = gelu_both(hidden)
        active = value.astype(BF)
        grad_hidden = (nt(grad_low, w2_ref[part]) * slope).astype(BF)
        bias = col_sum(grad_hidden)
        first = nn(norm_e_t, grad_hidden).astype(BF)
        for sub in range(chunk // width):
            row = index * (chunk // width) + sub
            small_ref[pl.ds(16 + row, 1)] = bias[:, width * sub : width * sub + width]
            at = pl.multiple_of(row * width, width)
            early_ref[slot[0], pl.ds(at, width)] = first[:, width * sub : width * sub + width]
        second = nn(grad_low_t, active).T.astype(BF)
        at = pl.multiple_of(jnp.where(index == 0, hidden_size, (index - 1) * chunk), chunk)
        early_ref[jnp.where(index == 0, slot[0], slot[1]), pl.ds(at, chunk)] = second
        return sums[0] + nn(active, w2_ref[part]), sums[1] + nt(grad_hidden, w1_ref[:, part])

    zeros = jnp.zeros((text, width), F32)
    feed_out, grad_norm = lax.fori_loop(0, hidden_size // chunk, feed, (zeros, zeros))
    y3 = y2 + b2_ref[1:2] + feed_out
    dec_ref[...] = jnp.where(valid, y3, 0.0).astype(BF)
    small_ref[4:5] = col_sum(grad)
    grad_x, small_ref[0:1], small_ref[1:2] = norm_backward(grad_norm, unit_e, scale_e, gain_ref[4:5])
    grad = grad + grad_x
    grad_low = grad.astype(BF)
    small_ref[5:6] = col_sum(grad_low)
    base = hidden_size - chunk
    early_ref[slot[1], base + 3 * width :] = nn(context_t.astype(BF), grad_low).astype(BF)
    grad_ctx = nt(grad_low, out2_ref[...]).astype(BF)
    turned[...] = cross_ref[:, :width].astype(F32).T.astype(BF)
    mem_t = mem_ref[...].astype(F32).T.astype(BF)
    grad_ref[...] = grad_ctx.astype(F32)

    def attend_backward(at, pair):
        queries = cross_q_ref[:, pl.ds(at, 128)] * jnp.asarray(HEAD_DIM**-0.5, BF)
        values = cross_ref[:, pl.ds(width + at, 128)]
        grads = grad_ref[:, pl.ds(at, 128)].astype(BF)
        dkey = 0.0
        dvalue = 0.0
        for odd in range(2):
            own_grad = own_lanes(grads, odd)
            prob = probs[2 * pair + odd]
            dprob = nt(values, own_grad)
            inner = jnp.sum(dprob * prob, axis=0, keepdims=True)
            dscore = (prob * (dprob - inner)).astype(BF)
            dvalue = dvalue + nn(prob.astype(BF), own_grad)
            dkey = dkey + nn(dscore, own_lanes(queries, odd))
            dq_t[head_rows(at, odd)] = nn(turned[head_rows(at, odd)], dscore)
        dkv[:, pl.ds(at, 128)] = dkey.astype(BF)
        dkv[:, pl.ds(width + at, 128)] = dvalue.astype(BF)

    each_pair(attend_backward)
    dq = (dq_t[...] * HEAD_DIM**-0.5).T.astype(BF)
    small_ref[6:7] = col_sum(dq)
    small_ref[7:8] = col_sum(dkv[:, width:])
    norm_d = norm_d_ref[...]
    early_ref[slot[1], base : base + width] = nn(norm_d.astype(F32).T.astype(BF), dq).astype(BF)
    pairs = nn(mem_t, dkv[...]).astype(BF)
    early_ref[slot[1], base + width : base + 2 * width] = pairs[:, :width]
    early_ref[slot[1], base + 2 * width : base + 3 * width] = pairs[:, width:]
    dmem_ref[...] = nt(dkv[...], in2_ref[:, width:]).astype(BF)
    unit, scale = normalise(y1_ref[...])
    grad_x, small_ref[8:9], small_ref[9:10] = norm_backward(
        nt(dq, in2_ref[:, :width]), unit, scale, gain_ref[3:4]
    )
    grad_ref[...] = grad + grad_x


def decoder_self_backward(
    emb_ref, norm_c_ref, qkv_ref, ctx_t_ref, prob_ref, grad_ref, small_ref, gain_ref, in1_ref, out1_ref,
    late_ref, swap_ref,
):
    text, width = emb_ref.shape
    grad = grad_ref[...]
    grad_low = grad.astype(BF)
    small_ref[10:11] = col_sum(grad_low)
    dout1 = nn(ctx_t_ref[...], grad_low).astype(BF)
    late_ref[3 * width :] = dout1[: width - SPILL]
    swap_ref[text + SMALL :] = dout1[width - SPILL :]
    grad_ctx = nt(grad_low, out1_ref[...]).astype(BF)
    key_t = qkv_ref[:, width : 2 * width].astype(F32).T.astype(BF)
    scaled = qkv_ref[:, :width] * jnp.asarray(HEAD_DIM**-0.5, BF)
    dkeys = []
    dvalues = []
    dquery = []
    for pair in range(HEADS // 2):
        dkey = 0.0
        dvalue = 0.0
        for head in (2 * pair, 2 * pair + 1):
            lanes = lanes_of(head)
            own_grad = own_lanes(grad_ctx[:, lanes], head)
            prob = prob_ref[head]
            dprob = nt(qkv_ref[:, slice(2 * width + lanes.start, 2 * width + lanes.stop)], own_grad)
            inner = jnp.sum(dprob * prob, axis=0, keepdims=True)
            dscore = (prob * (dprob - inner)).astype(BF)
            dvalue = dvalue + nn(prob.astype(BF), own_grad)
            dkey = dkey + nn(dscore, own_lanes(scaled[:, lanes], head))
            dquery.append(nn(key_t[rows_of(head)], dscore))
        dkeys.append(dkey.astype(BF))
        dvalues.append(dvalue.astype(BF))
    dq_t = jnp.concatenate(dquery, axis=0) * HEAD_DIM**-0.5
    dqkv = jnp.concatenate([dq_t.T.astype(BF)] + dkeys + dvalues, axis=1)
    small_ref[11:12] = col_sum(dqkv[:, :width])
    small_ref[12:13] = col_sum(dqkv[:, 2 * width :])
    din1 = nn(norm_c_ref[...].astype(F32).T.astype(BF), dqkv).astype(BF)
    for part in range(3):
        late_ref[width * part : width * part + width] = din1[:, width * part : width * part + width]
    unit, scale = normalise(emb_ref[...].astype(F32) * math.sqrt(width))
    grad_x, small_ref[13:14], small_ref[14:15] = norm_backward(
        nt(dqkv, in1_ref[...]), unit, scale, gain_ref[2:3]
    )
    swap_ref[:text] = ((grad + grad_x) * math.sqrt(width)).astype(BF)
    swap_ref[text : text + SMALL] = small_ref[...].astype(BF)


def forward_and_decoder(
    tok_ref, len_ref, at_ref, core_ref,
    x_ref, emb_ref, y1_ref, norm_c_ref, dec_qkv_ref, dec_ctx_t_ref, prob_ref, norm_d_ref, cross_q_ref,
    cot_ref, gain_ref, shift_ref, in_ref, in_b_ref, out_ref, out_b_ref, w1_from, b1_ref, w2_from, b2_ref,
    qkv_to, ctx_t_to, h1_to, lse_ref, dec_ref, dmem_ref, late_ref, swap_ref, keep_ref, send_ref,
    value_t, act, mem, cross, probs, cross_t, dkv, dq_t, grad, small, early, sems,
    w1_ref, w2_ref, qkv_ref, ctx_t_ref, h1_ref, load_sems, store_sems,
):
    loads = fetch(load_sems, (w1_from, w1_ref), (w2_from, w2_ref))
    stores = []

    def between():
        stores.extend(fetch(store_sems, (qkv_ref, qkv_to), (ctx_t_ref, ctx_t_to), (h1_ref, h1_to)))
        for load in loads:
            load.wait()

    in0, in1, in2 = (in_ref.at[i] for i in range(3))
    out0, out1, out2 = (out_ref.at[i] for i in range(3))
    encoder_forward(
        len_ref, at_ref, x_ref, gain_ref, shift_ref, in0, in_b_ref, out0, out_b_ref,
        w1_ref.at[0], b1_ref, w2_ref.at[0], b2_ref, in2,
        qkv_ref, ctx_t_ref, lse_ref, h1_ref, mem, cross,
        value_t, act, between,
    )
    decoder_main(
        tok_ref, len_ref, at_ref, core_ref,
        y1_ref, norm_d_ref, cross_q_ref, cross, mem, cot_ref, gain_ref, shift_ref,
        in2, out2, out_b_ref, w1_ref.at[1], b1_ref, w2_ref.at[1], b2_ref,
        dec_ref, dmem_ref, early, grad, small,
        probs, value_t, cross_t, dkv, dq_t,
    )
    decoder_self_backward(
        emb_ref, norm_c_ref, dec_qkv_ref, dec_ctx_t_ref, prob_ref, grad, small, gain_ref, in1, out1,
        late_ref, swap_ref,
    )
    half = early.shape[1]
    hand_out(
        sems, (early.at[0], keep_ref), (early.at[1], send_ref.at[:half]), (swap_ref, send_ref.at[half:])
    )
    for store in stores:
        store.wait()


def encoder_backward(
    len_ref, at_ref, core_ref,
    x_from, h1_ref, dmem_ref, ctx_t_ref, qkv_from, lse_ref, late_ref, gain_ref, shift_ref,
    in_from, out_ref, w1_ref, b1_ref, w2_ref,
    dx_ref, keep_ref, send_ref,
    grad_hid, dh1, dctx, key_t, dq_t, dqkv, small, feed, attn, sems,
    x_ref, qkv_ref, in_ref, load_sems, store_sems,
):
    loads = fetch(load_sems, (qkv_from, qkv_ref), (x_from, x_ref), (in_from.at[0], in_ref))
    encoder_feed_backward(
        core_ref, h1_ref, dmem_ref, ctx_t_ref, gain_ref, shift_ref, w1_ref, b1_ref, w2_ref, out_ref, late_ref,
        dh1, dctx, feed, small,
        grad_hid,
    )
    cut = feed.shape[1]
    stores = fetch(store_sems, (feed.at[0], keep_ref.at[:cut]), (feed.at[1], send_ref.at[:cut]))
    for load in loads:
        load.wait()
    encoder_attention_backward(
        len_ref, at_ref, core_ref, x_ref, qkv_ref, lse_ref, dctx, dh1, gain_ref, shift_ref, in_ref,
        dx_ref, attn,
        key_t, dq_t, dqkv, small,
    )
    hand_out(sems, (attn.at[0], keep_ref.at[cut:]), (attn.at[1], send_ref.at[cut:]))
    for store in stores:
        store.wait()


def fetch(sems, *pairs):
    copies = [pltpu.make_async_copy(ref, held, sems.at[i]) for i, (ref, held) in enumerate(pairs)]
    for copy in copies:
        copy.start()
    return copies


def early_merge(
    core_ref, ids_ref, swap_from, keep_ref, other_ref, out_ref, swap_ref, keep, other, swapped_ref, out, sems, out_sems
):
    core = core_ref[0]
    text = ids_ref.shape[1] // 2
    half = keep.shape[0]
    chunk = half // 4
    loads = fetch(
        sems, (swap_from, swap_ref), (other_ref.at[half:], swapped_ref), (keep_ref, keep),
        (other_ref.at[:half], other),
    )
    loads[0].wait()
    loads[1].wait()
    grad = jnp.concatenate([swap_ref[:text], swapped_ref[:text]], axis=0)
    for at in range(0, half, chunk):
        row = lax.broadcasted_iota(jnp.int32, (chunk, 2 * text), 0) + (core * half + at)
        hot = jnp.where(row == ids_ref[...], 1.0, 0.0).astype(BF)
        out[half + at : half + at + chunk] = nn(hot, grad).astype(BF)

    @pl.when(core == 1)
    def _():
        rest = swap_ref[text:].astype(F32) + swapped_ref[text:].astype(F32)
        out[2 * half - rest.shape[0] :] = rest.astype(BF)

    table = pltpu.make_async_copy(out.at[half:], out_ref.at[half:], out_sems.at[0])
    table.start()
    for load in loads[2:]:
        load.wait()
    out[:half] = (keep[...].astype(F32) + other[...].astype(F32)).astype(BF)
    sums = pltpu.make_async_copy(out.at[:half], out_ref.at[:half], out_sems.at[1])
    sums.start()
    table.wait()
    sums.wait()


def late_merge(keep_ref, other_ref, early_ref, out_ref, keep, other, early, out, sems, out_sems):
    count, size, width = out.shape
    size = size - early.shape[1]
    loads = fetch(sems, (early_ref, early), (keep_ref, keep), (other_ref, other))
    loads[0].wait()
    own = jnp.sum(early[...].astype(F32), axis=0).astype(BF)
    for load in loads[1:]:
        load.wait()
    stores = []
    part = count // 4
    for step in range(4):
        rows = slice(step * part * size, (step + 1) * part * size)
        places = slice(step * part, step * part + part)
        late = (keep[rows].astype(F32) + other[rows].astype(F32)).astype(BF)
        out[places, :size] = late.reshape(part, size, width)
        for place in range(step * part, step * part + part):
            out[place, size:] = own
        stores.append(pltpu.make_async_copy(out.at[places], out_ref.at[places], out_sems.at[step]))
        stores[-1].start()
    for store in stores:
        store.wait()


def late_spread(parts_ref, out_ref, parts, out, sems, out_sems):
    size = out.shape[1]
    half = out.shape[0] // 2
    ends = (slice(0, half), slice(half, 2 * half))
    loads = fetch(sems, *[(parts_ref.at[end, :size], parts.at[end]) for end in ends])
    total = 0.0
    for load, end in zip(loads, ends):
        load.wait()
        total = total + jnp.sum(parts[end].astype(F32), axis=0)
    late = total.astype(BF)
    stores = []
    for step, end in enumerate(ends):
        for place in range(end.start, end.stop):
            out[place] = late
        stores.append(pltpu.make_async_copy(out.at[end], out_ref.at[end], out_sems.at[step]))
        stores[-1].start()
    for store in stores:
        store.wait()


def early_outputs(core_ref, rate_ref, mine_ref, other_ref, table_ref, in_ref, out_ref, w1_ref, w2_ref, rest_ref):
    rate = rate_ref[0]
    first = core_ref[0] == 0
    count, size, width = mine_ref.shape
    blocks = w1_ref.shape[1] // width
    half = in_ref.shape[0] * 2 + w2_ref.shape[0]
    skip = size - 2 * half // count

    def rows(core, part):
        at = slice(count // 2 * part, count // 2 * (part + 1))
        mine, other = mine_ref[at, skip:], other_ref[at, skip:]
        picked = jnp.where(first, mine, other) if core == 0 else jnp.where(first, other, mine)
        return picked.reshape(half, width)

    table_ref[:half] = rows(0, 1).astype(F32) * rate
    rest = rows(1, 1)
    table_ref[half:] = rest[: table_ref.shape[0] - half].astype(F32) * rate
    rest_ref[...] = rest[half - rest_ref.shape[0] :]
    grads = jnp.concatenate([rows(0, 0), rows(1, 0)], axis=0).astype(F32) * rate
    for block in range(blocks):
        w1_ref[:, width * block : width * block + width] = grads[width * block : width * block + width]
    w2_ref[...] = grads[width * blocks : 2 * width * blocks]
    base = 2 * width * blocks
    for part in range(3):
        in_ref[:, width * part : width * part + width] = grads[base + width * part : base + width * part + width]
    out_ref[...] = grads[base + 3 * width :]


def late_outputs(
    half_ref, rate_ref, early_ref, rows_ref, in_in, out_in, w1_in, w2_in,
    in_ref, out_ref, w1_ref, w2_ref, rest_ref,
    rows, grads, sems, out_sems,
):
    size, width = rows.shape
    hidden = w2_ref.shape[1]
    cut = (width - SPILL) // 2
    base = hidden + 2 * width
    attn = base + cut
    over = size - attn - width
    (load,) = fetch(sems, (rows_ref, rows))
    load.wait()
    grads[:size] = rows[...].astype(F32) * rate_ref[0]
    grads[size:] = early_ref[SMALL:].astype(F32) * rate_ref[0]
    rest_ref[...] = rows[size - 2 * SMALL : size - SMALL]

    def block(at, rows=width):
        return grads.at[at : at + rows]

    def first():
        pairs = [(block(at), w1_ref.at[0, :, at : at + width]) for at in range(0, hidden, width)]
        pairs += [(block(hidden + at), in_ref.at[1, :, at : at + width]) for at in (0, width)]
        pairs.append((block(base, cut), out_ref.at[1, :cut]))
        pairs.append((block(attn), in_ref.at[0, :, :width]))
        pairs.append((block(attn + width, over), in_ref.at[0, :over, width : 2 * width]))
        return pairs

    def second():
        pairs = [(block(0, hidden), w2_ref.at[0])]
        pairs.append((block(hidden), in_ref.at[1, :, 2 * width :]))
        pairs.append((block(hidden + width), out_ref.at[0]))
        pairs.append((block(base, cut), out_ref.at[1, cut : 2 * cut]))
        pairs.append((block(size, SPILL), out_ref.at[1, 2 * cut :]))
        pairs.append((block(attn, width - over), in_ref.at[0, over:, width : 2 * width]))
        pairs.append((block(attn + width - over), in_ref.at[0, :, 2 * width :]))
        return pairs

    @pl.when(half_ref[0] == 0)
    def _():
        hand_out(out_sems, *first())

    @pl.when(half_ref[0] == 1)
    def _():
        hand_out(out_sems, *second())


def small_outputs(
    core_ref, rate_ref, mine_ref, other_ref, early_ref,
    gain_ref, shift_ref, in_b_ref, out_b_ref, b1_ref, b2_ref,
):
    width = mine_ref.shape[1]
    rate = rate_ref[0]
    enc = jnp.where(core_ref[0] == 1, mine_ref[...], other_ref[...]).astype(F32) * rate
    dec = early_ref[:SMALL].astype(F32) * rate
    for row, (part, at) in enumerate(((enc, 0), (enc, 8), (dec, 13), (dec, 8), (dec, 0))):
        gain_ref[row : row + 1] = part[at : at + 1]
        shift_ref[row : row + 1] = part[at + 1 : at + 2]
    for row, (part, at, next_at) in enumerate(((enc, 2, 3), (dec, 11, 12), (dec, 6, 7))):
        in_b_ref[row : row + 1, :width] = part[at : at + 1]
        in_b_ref[row : row + 1, width:] = part[next_at : next_at + 1]
    for row, (part, at) in enumerate(((enc, 11), (dec, 10), (dec, 5))):
        out_b_ref[row : row + 1] = part[at : at + 1]
    for row, (part, at) in enumerate(((enc, 10), (dec, 4))):
        b2_ref[row : row + 1] = part[at : at + 1]
    for row, part in enumerate((enc, dec)):
        for block in range(b1_ref.shape[1] // width):
            b1_ref[row : row + 1, width * block : width * block + width] = part[16 + block : 17 + block]


def frames_back(place_ref, own_ref, next_ref, second_ref, third_ref, out_ref):
    count = out_ref.shape[0]
    for shift, ref in enumerate((own_ref, next_ref, second_ref, third_ref)):
        out_ref[lax.rem(place_ref[0] + (count - shift), count)] = ref[...].astype(F32)


def encoder_feed_backward(
    core_ref, h1_ref, dmem_ref, ctx_t_ref, gain_ref, shift_ref, w1_ref, b1_ref, w2_ref, out_ref, late_ref,
    dh1_ref, dctx_ref, feed_ref, small_ref,
    grad_hid,
):
    width = h1_ref.shape[1]
    hidden_size = w1_ref.shape[1]
    slot = (core_ref[0], 1 - core_ref[0])
    cut = (width - SPILL) // 2
    feed_ref[slot[0], hidden_size : hidden_size + 2 * width] = late_ref[: 2 * width]
    feed_ref[slot[1], hidden_size : hidden_size + width] = late_ref[2 * width : 3 * width]
    feed_ref[slot[0], hidden_size + 2 * width :] = late_ref[3 * width : 3 * width + cut]
    feed_ref[slot[1], hidden_size + 2 * width :] = late_ref[3 * width + cut :]
    small_ref[...] = jnp.zeros_like(small_ref)
    unit, _ = normalise(h1_ref[...])
    norm_b = unit * gain_ref[1:2] + shift_ref[1:2]
    norm_b_t = norm_b.T.astype(BF)
    norm_b = norm_b.astype(BF)
    grad_low = dmem_ref[...]
    grad_low_t = grad_low.astype(F32).T.astype(BF)
    chunk = FEED_CHUNK

    def feed(index, carry):
        part = pl.ds(pl.multiple_of(index * chunk, chunk), chunk)
        hidden = nn(norm_b, w1_ref[:, part]) + b1_ref[0:1, part]
        value, slope = gelu_both(hidden)
        grad_hidden = (nt(grad_low, w2_ref[part]) * slope).astype(BF)
        grad_hid[:, part] = grad_hidden
        bias = col_sum(grad_hidden)
        first = nn(norm_b_t, grad_hidden).astype(BF)
        for sub in range(chunk // width):
            row = index * (chunk // width) + sub
            small_ref[pl.ds(16 + row, 1)] = bias[:, width * sub : width * sub + width]
            at = pl.multiple_of(row * width, width)
            feed_ref[slot[0], pl.ds(at, width)] = first[:, width * sub : width * sub + width]
        feed_ref[slot[1], part] = nn(grad_low_t, value.astype(BF)).T.astype(BF)
        return carry

    lax.fori_loop(0, hidden_size // chunk, feed, 0)
    grad = grad_low.astype(F32)
    small_ref[10:11] = col_sum(grad)
    unit, scale = normalise(h1_ref[...])
    grad_x, small_ref[8:9], small_ref[9:10] = norm_backward(
        nt(grad_hid[...], w1_ref[...]), unit, scale, gain_ref[1:2]
    )
    grad = grad + grad_x
    dh1_ref[...] = grad
    grad_low = grad.astype(BF)
    small_ref[11:12] = col_sum(grad_low)
    feed_ref[slot[1], hidden_size + width : hidden_size + 2 * width] = nn(ctx_t_ref[...], grad_low).astype(BF)
    dctx_ref[...] = nt(grad_low, out_ref[...]).astype(BF)


def encoder_attention_backward(
    len_ref, at_ref, core_ref, x_ref, qkv_ref, lse_ref, dctx_ref, dh1_ref, gain_ref, shift_ref, in_ref,
    dx_ref, attn_ref,
    key_t, dq_t, dqkv, small_ref,
):
    rows, width = x_ref.shape
    key_t[...] = qkv_ref[:, width : 2 * width].astype(F32).T.astype(BF)

    def attend_backward(at, pair):
        keys = qkv_ref[:, pl.ds(width + at, 128)]
        values = qkv_ref[:, pl.ds(2 * width + at, 128)]
        queries = qkv_ref[:, pl.ds(at, 128)] * jnp.asarray(HEAD_DIM**-0.5, BF)
        grads = dctx_ref[:, pl.ds(at, 128)]
        dkey = 0.0
        dvalue = 0.0
        for odd in range(2):
            query = own_lanes(queries, odd)
            score = nt(with_mask(keys, odd, len_ref[at_ref[0]]), with_one(query, odd))
            prob = jnp.exp(score - lse_ref[pl.ds(2 * pair + odd, 1)])
            own_grad = own_lanes(grads, odd)
            dprob = nt(values, own_grad)
            inner = jnp.sum(dprob * prob, axis=0, keepdims=True)
            dscore = (prob * (dprob - inner)).astype(BF)
            dkey = dkey + nn(dscore, query)
            dvalue = dvalue + nn(prob.astype(BF), own_grad)
            dq_t[head_rows(at, odd)] = nn(key_t[head_rows(at, odd)], dscore)
        dqkv[:, pl.ds(width + at, 128)] = dkey.astype(BF)
        dqkv[:, pl.ds(2 * width + at, 128)] = dvalue.astype(BF)

    each_pair(attend_backward)
    dqkv[:, :width] = (dq_t[...].T * HEAD_DIM**-0.5).astype(BF)
    small_ref[2:3] = col_sum(dqkv[:, :width])
    small_ref[3:4] = col_sum(dqkv[:, 2 * width :])
    unit, scale = normalise(x_ref[...].astype(F32))
    norm_a = unit * gain_ref[0:1] + shift_ref[0:1]
    din = nn(norm_a.T.astype(BF), dqkv[...]).astype(BF)
    blocks = [din[:, width * part : width * part + width] for part in range(3)]
    grad_x, small_ref[0:1], small_ref[1:2] = norm_backward(
        nt(dqkv[...], in_ref[...]), unit, scale, gain_ref[0:1]
    )
    dx_ref[...] = (dh1_ref[...] + grad_x).astype(BF)
    small = small_ref[...].astype(BF)
    packed = jnp.concatenate(blocks + [small, jnp.zeros_like(small)], axis=0)
    half = attn_ref.shape[1]
    attn_ref[core_ref[0]] = packed[:half]
    attn_ref[1 - core_ref[0]] = packed[half:]


def swap_cores(array):
    return lax.ppermute(array, "core", [(0, 1), (1, 0)])


def body(
    frames, utt_len, token_ids, tok_len, step, embed, norm_gain, norm_bias, attn_in, attn_in_bias,
    attn_out, attn_out_bias, ff_in, ff_in_bias, ff_out, ff_out_bias, cotangent,
):
    ring = ("frame", "pair")
    devices = lax.axis_size(ring)
    core = lax.axis_index("core")
    core_of = core[None]
    frame_at = lax.axis_index("frame")
    vocab, width = embed.shape
    hidden = ff_in.shape[2]
    frame_count = lax.axis_size("frame")
    local_len = frames.shape[2]
    rows = local_len * frame_count
    text = token_ids.shape[2]
    lengths = utt_len[0]
    frame_of = frame_at[None]
    my_tok = tok_len[0]
    arrived = lax.all_to_all(frames[0], "frame", split_axis=0, concat_axis=1, tiled=True)
    source = arrived.reshape(rows, width)
    ids = token_ids[0, 0]
    both_ids = jnp.concatenate([ids, swap_cores(ids)])[None]
    rows_in, both_ids = lax.optimization_barrier((embed[ids], both_ids))
    count_step = step[0].astype(F32)
    rate = jnp.minimum(lax.rsqrt(count_step), count_step * WARMUP ** (-1.5)) * WARMUP**0.5
    rate = rate[None]

    y1, norm_c, dec_qkv, dec_ctx_t, dec_prob, norm_d, cross_q = call(
        decoder_start,
        [
            ((text, width), F32), ((text, width), BF), ((text, 3 * width), BF), ((width, text), BF),
            ((HEADS, text, text), F32), ((text, width), BF), ((text, width), BF),
        ],
        [
            rows_in, norm_gain, norm_bias, (attn_in, 1), attn_in_bias, (attn_out, 1),
            attn_out_bias, (attn_in, 2),
        ],
        [my_tok],
        flops=2 * text * width * width * 5,
    )
    half = 2 * width + hidden
    swap_rows = text + SMALL + SPILL
    enc_qkv, enc_ctx_t, h1, lse, dec_out, dmem, self_grads, swap, early, early_send = call(
        forward_and_decoder,
        [
            ((rows, 3 * width), BF, None), ((width, rows), BF, None), ((rows, width), F32, None),
            ((8, rows), F32), ((text, width), BF), ((rows, width), BF), ((4 * width - SPILL, width), BF),
            ((swap_rows, width), BF), ((half, width), BF, None), ((half + swap_rows, width), BF, None),
        ],
        [
            source, rows_in, y1, norm_c, dec_qkv, dec_ctx_t, dec_prob, norm_d, cross_q, cotangent[0, 0],
            norm_gain, norm_bias, attn_in, attn_in_bias, attn_out, attn_out_bias, (ff_in, None), ff_in_bias,
            (ff_out, None), ff_out_bias,
        ],
        [my_tok, lengths, frame_of, core_of],
        [
            pltpu.VMEM((width, rows), BF), pltpu.VMEM((rows, hidden), BF), pltpu.VMEM((rows, width), BF),
            pltpu.VMEM((rows, 2 * width), BF), pltpu.VMEM((HEADS, rows, text), F32),
            pltpu.VMEM((width, text), F32), pltpu.VMEM((rows, 2 * width), BF),
            pltpu.VMEM((width, text), F32), pltpu.VMEM((text, width), F32),
            pltpu.VMEM((SMALL, width), F32), pltpu.VMEM((2, half, width), BF),
            pltpu.SemaphoreType.DMA((3,)),
            pltpu.VMEM(ff_in.shape, BF), pltpu.VMEM(ff_out.shape, BF), pltpu.VMEM((rows, 3 * width), BF),
            pltpu.VMEM((width, rows), BF), pltpu.VMEM((rows, width), F32),
            pltpu.SemaphoreType.DMA((2,)), pltpu.SemaphoreType.DMA((3,)),
        ],
        flops=2 * rows * width * (10 * width + 2 * rows + 2 * hidden)
        + 2 * text * width * (6 * hidden + 7 * rows + 26 * width),
    )
    (early_sum,) = call(
        early_merge,
        [((2 * half, width), BF, None)],
        [both_ids, (swap, None), (early, None), (swap_cores(early_send), "vmem")],
        [core_of],
        [
            pltpu.VMEM((swap_rows, width), BF), pltpu.VMEM((half, width), BF), pltpu.VMEM((half, width), BF),
            pltpu.VMEM((swap_rows, width), BF), pltpu.VMEM((2 * half, width), BF),
            pltpu.SemaphoreType.DMA((4,)), pltpu.SemaphoreType.DMA((2,)),
        ],
        flops=4 * half * width * text,
        limit=20,
    )
    early_sum, dmem = lax.optimization_barrier((early_sum, dmem))
    early_parts = lax.all_to_all(
        early_sum.reshape(devices, -1, width), ring, split_axis=0, concat_axis=0, tiled=True
    )
    early_own = jnp.sum(early_parts.astype(F32), axis=0).astype(BF)

    feed_half = (5 * width - SPILL) // 2 + hidden
    attn_half = 3 * width // 2 + SMALL
    late_half = feed_half + attn_half
    dx, late, late_send = call(
        encoder_backward,
        [((rows, width), BF), ((late_half, width), BF, None), ((late_half, width), BF, None)],
        [
            (source, None), h1, dmem, enc_ctx_t, (enc_qkv, None), lse, self_grads, norm_gain, norm_bias,
            (attn_in, None), (attn_out, 0), (ff_in, 0), ff_in_bias, (ff_out, 0),
        ],
        [lengths, frame_of, core_of],
        [
            pltpu.VMEM((rows, hidden), BF), pltpu.VMEM((rows, width), F32), pltpu.VMEM((rows, width), BF),
            pltpu.VMEM((width, rows), BF), pltpu.VMEM((width, rows), F32), pltpu.VMEM((rows, 3 * width), BF),
            pltpu.VMEM((SMALL, width), F32), pltpu.VMEM((2, feed_half, width), BF),
            pltpu.VMEM((2, attn_half, width), BF), pltpu.SemaphoreType.DMA((2,)),
            pltpu.VMEM((rows, width), BF), pltpu.VMEM((rows, 3 * width), BF), pltpu.VMEM((width, 3 * width), BF),
            pltpu.SemaphoreType.DMA((3,)), pltpu.SemaphoreType.DMA((2,)),
        ],
        flops=2 * rows * width * (5 * hidden + 5 * rows + 8 * width),
    )
    late_size = late_half // devices
    early_size = 2 * half // devices
    mixed_shape = (devices, late_size + early_size, width)
    (mixed,) = call(
        late_merge,
        [(mixed_shape, BF, None)],
        [(late, None), (swap_cores(late_send), None), (early_parts, None)],
        scratch=[
            pltpu.VMEM((late_half, width), BF), pltpu.VMEM((late_half, width), BF),
            pltpu.VMEM((devices, early_size, width), BF), pltpu.VMEM(mixed_shape, BF),
            pltpu.SemaphoreType.DMA((3,)), pltpu.SemaphoreType.DMA((4,)),
        ],
        limit=24,
    )
    mixed = lax.all_to_all(mixed, ring, split_axis=0, concat_axis=0, tiled=True)
    chunks = dx.reshape(frame_count, local_len, width)
    moved = []
    for shift in range(frame_count):
        target = lax.rem(frame_at + shift, frame_count)
        chunk = lax.dynamic_index_in_dim(chunks, target, keepdims=False)
        if shift:
            chunk = lax.ppermute(chunk, "frame", [(i, (i + shift) % frame_count) for i in range(frame_count)])
        moved.append(chunk)
    mixed, moved = lax.optimization_barrier((mixed, moved))
    late_shape = (devices, late_size, width)
    (late_own,) = call(
        late_spread,
        [(late_shape, BF, None)],
        [(mixed, None)],
        scratch=[
            pltpu.VMEM(late_shape, BF), pltpu.VMEM(late_shape, BF),
            pltpu.SemaphoreType.DMA((2,)), pltpu.SemaphoreType.DMA((2,)),
        ],
    )
    early_other = swap_cores(mixed)
    (frames_grad,) = call(
        frames_back, [((frame_count, local_len, width), F32)], moved, [frame_of], limit=16
    )
    late_mine = lax.all_to_all(late_own, ring, split_axis=0, concat_axis=0, tiled=True)
    in_shape = (3, width, 3 * width)
    out_shape = (3, width, width)
    w1_shape = (2, width, hidden)
    w2_shape = (2, hidden, width)
    table_grad, in_grad, out_grad, w1_grad, w2_grad, early_rest = call(
        early_outputs,
        [
            ((vocab, width), F32), (in_shape, F32, None, 2), (out_shape, F32, None, 2),
            (w1_shape, F32, None, 1), (w2_shape, F32, None, 1), ((SMALL + SPILL, width), BF),
        ],
        [mixed, early_other],
        [core_of, rate],
        limit=40,
    )
    late_mine, early_rest, frames_grad = lax.optimization_barrier((late_mine, early_rest, frames_grad))
    late_mine = late_mine.reshape(late_half, width)
    late_other = swap_cores(late_mine)
    results = (in_grad, out_grad, w1_grad, w2_grad)
    rests = []
    for rows_of_half, which in ((late_mine, core_of), (late_other, 1 - core_of)):
        *results, rest = call(
            late_outputs,
            [
                (in_shape, F32, None), (out_shape, F32, None), (w1_shape, F32, None),
                (w2_shape, F32, None), ((SMALL, width), BF),
            ],
            [early_rest, (rows_of_half, "vmem")] + [(result, None) for result in results],
            [which, rate],
            [
                pltpu.VMEM((late_half, width), BF), pltpu.VMEM((late_half + SPILL, width), F32),
                pltpu.SemaphoreType.DMA((1,)), pltpu.SemaphoreType.DMA((16,)),
            ],
            aliases={4: 0, 5: 1, 6: 2, 7: 3},
            limit=16,
        )
        rests.append(rest)
    in_grad, out_grad, w1_grad, w2_grad = results
    gain_grad, shift_grad, in_b_grad, out_b_grad, b1_grad, b2_grad = call(
        small_outputs,
        [
            ((5, width), F32), ((5, width), F32), ((3, 2 * width), F32), ((3, width), F32),
            ((2, hidden), F32), ((2, width), F32),
        ],
        rests + [early_rest],
        [core_of, rate],
        limit=32,
    )
    return (
        dec_out[None, None],
        frames_grad[None],
        table_grad,
        gain_grad,
        shift_grad,
        in_grad,
        in_b_grad,
        out_grad,
        out_b_grad,
        w1_grad,
        b1_grad,
        w2_grad,
        b2_grad,
    )


def solution(mesh):
    groups = ("pair", "core")
    frames, batch = mesh.devices.shape
    split = Mesh(mesh.devices.reshape(frames, batch // 2, 2), ("frame",) + groups)
    placed = (
        P(groups, None, "frame", None),
        P(groups, None),
        P(groups, "frame", None),
        P(groups, "frame"),
    ) + (P(),) * 12 + (P(groups, "frame", None, None),)
    results = (P(groups, "frame", None, None), P(groups, None, "frame", None)) + (P(),) * 11
    return jax.shard_map(body, mesh=split, in_specs=placed, out_specs=results, check_vma=False)
```

profile of v0, /device:TPU:1, one launch (start us, length us, event | category | flops | bytes accessed | tf_op | source)
XLA Modules:
  0.0 208.6 jit_solution(3819388635700410831)
XLA Ops:
  0.6 0.0 copy-start
  0.7 6.0 %all-to-all-start = ((bf16[4,256,256]{2,1,0:T(8,128)(2,1)}), bf16[4,256,256]{2,1,0:T(8,128)(2,1)}, u32[]{:S(2)}, u32[]{:S(2)}) async-start(bf16[4,256,256]{2,1,0:T(8,128)(2,1)} %bitcast.31), calls=%async_computation | async-start | bytes 1048576 | tf_op jit(solution)/shard_map/all_to_all | solution.py:782
  6.7 1.0 collective-permute-start
  7.6 0.7 fusion
  8.9 0.0 copy-done
  8.9 1.5 gather_fusion
  10.4 0.0 collective-permute-done
  10.4 0.7 pad_add_fusion
  11.1 3.3 %decoder_start.1 = (f32[128,256]{1,0:T(8,128)}, bf16[128,256]{1,0:T(8,128)(2,1)}, bf16[128,768]{1,0:T(8,128)(2,1)}, bf16[256,128]{1,0:T(8,128)(2,1)}, f32[4,128,...) custom-call(s32[1]{0:T(128)} %bitcast.26.tok_ref, bf16[128,256]{1,0:T(8,128)(2,1)} %gather_fusion, ...), custom_call_target="tpu_custom_call" | custom-call | flops 83886080 | bytes 3689472 | tf_op jit(solution)/shard_map/decoder_start/pallas_call | solution.py:142
  14.4 0.7 all-to-all-done
  15.0 27.7 %forward_and_decoder.1 = (bf16[1024,768]{1,0:T(8,128)(2,1)}, bf16[256,1024]{1,0:T(8,128)(2,1)}, f32[1024,256]{1,0:T(8,128)}, f32[8,1024]{1,0:T(8,128)}, bf16[128...) custom-call(s32[1]{0:T(128)} %bitcast.27.tok_ref, ...), custom_call_target="tpu_custom_call" | custom-call | flops 6274678784 | bytes 14423040 | tf_op jit(solution)/shard_map/forward_and_decoder/pallas_call | solution.py:142
  42.8 2.2 %collective-permute-start.1 = (bf16[2784,256]{1,0:T(8,128)(2,1)}, bf16[2784,256]{1,0:T(8,128)(2,1)S(1)}, u32[]{:S(2)}, u32[]{:S(2)}) collective-permute-start(bf16[2784,256]{1,0:T(8,128)(2,1)} %get-tuple-element.80), channel_id=1, source_target_pairs={{0,1},{1,0},{2,3},{3,2},{4,5},{5,4},{6,7},{7,6},{8,9},{9,8},{10,11... | collective-permute-start | bytes 4276232 | tf_op jit(solution)/shard_map/ppermute | solution.py:761
  45.0 3.0 %collective-permute-done.1.other_ref = bf16[2784,256]{1,0:T(8,128)(2,1)S(1)} collective-permute-done((bf16[2784,256]{1,0:T(8,128)(2,1)}, bf16[2784,256]{1,0:T(8,128)(2,1)S(1)}, u32[]{:S(2)}, u32[]{:S(2)}) %collective-permute-start.1) | collective-permute-done | bytes 1425440 | tf_op jit(solution)/shard_map/ppermute | solution.py:761
  48.1 3.0 %early_merge.1 = bf16[5120,256]{1,0:T(8,128)(2,1)} custom-call(s32[1]{0:T(128)} %bitcast.3.core_ref.half_ref, s32[1,256]{1,0:T(1,128)S(1)} %bitcast.28, bf16[224,256]{1,0:T(8,128)(2,1)} %get-tuple-element.78.swap_from, bf16[2560,256]{1,0:T(8,128)(2,1)} %get-tuple-element.79.keep_ref, bf16[2784,256]{1,0:T(8,128)(2,1)S(1)} %collective-permute-done.1.other_ref), custom_call_target="tpu_custom_call" | custom-call | flops 335544320 | bytes 5473280 | tf_op jit(solution)/shard_map/early_merge/pallas_call | solution.py:142
  51.0 8.5 %all-to-all-start.1 = ((bf16[64,80,256]{2,1,0:T(8,128)(2,1)}), bf16[64,80,256]{2,1,0:T(8,128)(2,1)}, u32[]{:S(2)}, u32[]{:S(2)}) async-start(bf16[64,80,256]{2,1,0:T(8,128)(2,1)} %bitcast.29), calls=%async_computation.1 | async-start | bytes 5242880 | tf_op jit(solution)/shard_map/all_to_all | solution.py:847
  59.5 31.3 %encoder_backward.1 = (bf16[1024,256]{1,0:T(8,128)(2,1)}, bf16[3072,256]{1,0:T(8,128)(2,1)}, bf16[3072,256]{1,0:T(8,128)(2,1)}) custom-call(s32[4]{0:T(128)} %bitcast.37, s32[1]{0:T(128)} %bitcast.2.at_ref.place_ref, s32[1]{0:T(128)} %bitcast.3.core_ref.half_ref, bf16[1024,256]{1,0:T(8,128)(2,1)} %bitcast.5.x_ref.x_from, ...), custom_call_target="tpu_custom_call" | custom-call | flops 9126805504 | bytes 14182400 | tf_op jit(solution)/shard_map/encoder_backward/pallas_call | solution.py:142
  90.8 0.7 collective-permute-start.2
  91.6 3.4 %collective-permute-done.2.other_ref = bf16[3072,256]{1,0:T(8,128)(2,1)} collective-permute-done((bf16[3072,256]{1,0:T(8,128)(2,1)}, bf16[3072,256]{1,0:T(8,128)(2,1)}, u32[]{:S(2)}, u32[]{:S(2)}) %collective-permute-start.2) | collective-permute-done | bytes 1572896 | tf_op jit(solution)/shard_map/ppermute | solution.py:761
  94.9 0.0 all-to-all-done.1.early_ref
  94.9 4.9 %late_merge.1 = bf16[64,128,256]{2,1,0:T(8,128)(2,1)} custom-call(bf16[3072,256]{1,0:T(8,128)(2,1)} %get-tuple-element.87.keep_ref, bf16[3072,256]{1,0:T(8,128)(2,1)} %collective-permute-done.2.other_ref, bf16[64,80,256]{2,1,0:T(8,128)(2,1)} %all-to-all-done.1.early_ref), custom_call_target="tpu_custom_call" | custom-call | bytes 9961472 | tf_op jit(solution)/shard_map/late_merge/pallas_call | solution.py:142
  99.8 10.3 %all-to-all-start.2 = ((bf16[64,128,256]{2,1,0:T(8,128)(2,1)}), bf16[64,128,256]{2,1,0:T(8,128)(2,1)}, u32[]{:S(2)}, u32[]{:S(2)}) async-start(bf16[64,128,256]{2,1,0:T(8,128)(2,1)} %late_merge.1), calls=%async_computation.2 | async-start | bytes 8388608 | tf_op jit(solution)/shard_map/all_to_all | solution.py:887
  110.1 1.1 dynamic-slice_bitcast_fusion
  111.3 2.4 %collective-permute-start.5 = (bf16[256,256]{1,0:T(8,128)(2,1)S(1)}, bf16[256,256]{1,0:T(8,128)(2,1)S(1)}, u32[]{:S(2)}, u32[]{:S(2)}) collective-permute-start(bf16[256,256]{1,0:T(8,128)(2,1)S(1)} %get-tuple-element.121), channel_id=1, source_target_pairs={{0,96},{32,0},{64,32},{96,64},{1,97},{33,1},{65,33},{97,65},{2,98}... | collective-permute-start | bytes 393224 | tf_op jit(solution)/shard_map/ppermute | solution.py:894
  113.7 0.4 collective-permute-start.4
  114.1 0.7 collective-permute-start.3
  114.8 32.2 %collective-permute-done.5.third_ref = bf16[256,256]{1,0:T(8,128)(2,1)S(1)} collective-permute-done((bf16[256,256]{1,0:T(8,128)(2,1)S(1)}, bf16[256,256]{1,0:T(8,128)(2,1)S(1)}, u32[]{:S(2)}, u32[]{:S(2)}) %collective-permute-start.5) | collective-permute-done | bytes 131104 | tf_op jit(solution)/shard_map/ppermute | solution.py:894
  146.9 0.0 collective-permute-done.4.second_ref
  146.9 14.4 %collective-permute-done.3.next_ref = bf16[256,256]{1,0:T(8,128)(2,1)S(1)} collective-permute-done((bf16[256,256]{1,0:T(8,128)(2,1)S(1)}, bf16[256,256]{1,0:T(8,128)(2,1)S(1)}, u32[]{:S(2)}, u32[]{:S(2)}) %collective-permute-start.3) | collective-permute-done | bytes 131104 | tf_op jit(solution)/shard_map/ppermute | solution.py:894
  161.3 0.0 copy-start.1
  161.3 0.7 copy-done.1
  162.0 1.1 all-to-all-done.2.parts_ref.mine_ref
  163.1 2.4 %collective-permute-start.6 = (bf16[64,128,256]{2,1,0:T(8,128)(2,1)}, bf16[64,128,256]{2,1,0:T(8,128)(2,1)}, u32[]{:S(2)}, u32[]{:S(2)}) collective-permute-start(bf16[64,128,256]{2,1,0:T(8,128)(2,1)} %all-to-all-done.2.parts_ref.mine_ref), channel_id=1, source_target_pairs={{0,1},{1,0},{2,3},{3,2},{4,5},{5,4},{6,7},{7,6},{8,9},{9,8},{10,11... | collective-permute-start | bytes 12582920 | tf_op jit(solution)/shard_map/ppermute | solution.py:761
  165.5 2.7 %late_spread.1 = bf16[64,48,256]{2,1,0:T(8,128)(2,1)} custom-call(bf16[64,128,256]{2,1,0:T(8,128)(2,1)} %all-to-all-done.2.parts_ref.mine_ref), custom_call_target="tpu_custom_call" | custom-call | bytes 5767168 | tf_op jit(solution)/shard_map/late_spread/pallas_call | solution.py:142
  168.2 0.0 copy-start.2
  168.2 8.8 %all-to-all-start.3 = ((bf16[64,48,256]{2,1,0:T(8,128)(2,1)}), bf16[64,48,256]{2,1,0:T(8,128)(2,1)}, u32[]{:S(2)}, u32[]{:S(2)}) async-start(bf16[64,48,256]{2,1,0:T(8,128)(2,1)} %late_spread.1), calls=%async_computation.3 | async-start | bytes 3145728 | tf_op jit(solution)/shard_map/all_to_all | solution.py:911
  177.7 0.0 copy-done.2
  177.7 1.0 frames_back.1
  178.7 0.0 collective-permute-done.6.other_ref
  178.7 7.6 %early_outputs.1 = (f32[5000,256]{1,0:T(8,128)}, f32[3,256,768]{2,1,0:T(8,128)}, f32[3,256,256]{2,1,0:T(8,128)}, f32[2,256,2048]{2,1,0:T(8,128)}, f32[2,2048,256]{2,1,0:T(8,128)}, /*index=5*/bf16[96,256]{1,0:T(8,128)(2,1)S(1)}) custom-call(s32[1]{0:T(128)} %bitcast.3.core_ref.half_ref, f32[1]{0:T(128)S(6)} %mul.9.rate_ref, ...), custom_call_target="tpu_custom_call" | custom-call | bytes 25092096 | tf_op jit(solution)/shard_map/early_outputs/pallas_call | solution.py:142
  186.4 14.0 %all-to-all-done.3 = bf16[64,48,256]{2,1,0:T(8,128)(2,1)} async-done(((bf16[64,48,256]{2,1,0:T(8,128)(2,1)}), bf16[64,48,256]{2,1,0:T(8,128)(2,1)}, u32[]{:S(2)}, u32[]{:S(2)}) %all-to-all-start.3) | async-done | bytes 1572896 | tf_op jit(solution)/shard_map/all_to_all | solution.py:911
  200.4 1.6 collective-permute-start.7
  202.0 3.4 %late_outputs.2 = (f32[3,256,768]{2,1,0:T(8,128)}, f32[3,256,256]{2,1,0:T(8,128)}, f32[2,256,2048]{2,1,0:T(8,128)}, f32[2,2048,256]{2,1,0:T(8,128)}, bf16[32,256]{1,0:T(8,128)(2,1)S(1)}) custom-call(s32[1]{0:T(128)} %bitcast.3.core_ref.half_ref, f32[1]{0:T(128)S(6)} %mul.9.rate_ref, ...), custom_call_target="tpu_custom_call", output_to_operand_aliasing={{0}: (4, {}), {1}: (5, {}), {2}: (6, {}), {3}: (7, {})} | custom-call | bytes 24707072 | tf_op jit(solution)/shard_map/late_outputs/pallas_call | solution.py:142
  205.4 0.0 collective-permute-done.7.rows_ref
  205.4 2.1 %late_outputs.3 = (f32[3,256,768]{2,1,0:T(8,128)}, f32[3,256,256]{2,1,0:T(8,128)}, f32[2,256,2048]{2,1,0:T(8,128)}, f32[2,2048,256]{2,1,0:T(8,128)}, bf16[32,256]{1,0:T(8,128)(2,1)S(1)}) custom-call(s32[1]{0:T(128)S(6)} %sub.3.half_ref, f32[1]{0:T(128)S(6)} %mul.9.rate_ref, ...), custom_call_target="tpu_custom_call", output_to_operand_aliasing={{0}: (4, {}), {1}: (5, {}), {2}: (6, {}), {3}: (7, {})} | custom-call | bytes 24707072 | tf_op jit(solution)/shard_map/late_outputs/pallas_call | solution.py:142
  207.6 0.6 small_outputs.1
  (1 shorter events, 0.0 us)
Async XLA Ops:
  0.6 8.3 %copy-start = (bf16[5000,256]{1,0:T(8,128)(2,1)S(1)}, bf16[5000,256]{1,0:T(8,128)(2,1)}, u32[]{:S(2)}) copy-start(bf16[5000,256]{1,0:T(8,128)(2,1)} %param.22) | copy-start | bytes 7680004
  0.7 14.4 %all-to-all-start = ((bf16[4,256,256]{2,1,0:T(8,128)(2,1)}), bf16[4,256,256]{2,1,0:T(8,128)(2,1)}, u32[]{:S(2)}, u32[]{:S(2)}) async-start(bf16[4,256,256]{2,1,0:T(8,128)(2,1)} %bitcast.31), calls=%async_computation | async-start | bytes 1048576 | tf_op jit(solution)/shard_map/all_to_all | solution.py:782
  6.7 3.8 %collective-permute-start = (s32[128]{0:T(128)}, s32[128]{0:T(128)S(1)}, u32[]{:S(2)}, u32[]{:S(2)}) collective-permute-start(s32[128]{0:T(128)} %bitcast.33), channel_id=1, source_target_pairs={{0,1},{1,0},{2,3},{3,2},{4,5},{5,4},{6,7},{7,6},{8,9},{9,8},{10,11... | collective-permute-start | bytes 1544 | tf_op jit(solution)/shard_map/ppermute | solution.py:761
  42.8 5.3 %collective-permute-start.1 = (bf16[2784,256]{1,0:T(8,128)(2,1)}, bf16[2784,256]{1,0:T(8,128)(2,1)S(1)}, u32[]{:S(2)}, u32[]{:S(2)}) collective-permute-start(bf16[2784,256]{1,0:T(8,128)(2,1)} %get-tuple-element.80), channel_id=1, source_target_pairs={{0,1},{1,0},{2,3},{3,2},{4,5},{5,4},{6,7},{7,6},{8,9},{9,8},{10,11... | collective-permute-start | bytes 4276232 | tf_op jit(solution)/shard_map/ppermute | solution.py:761
  51.0 43.9 %all-to-all-start.1 = ((bf16[64,80,256]{2,1,0:T(8,128)(2,1)}), bf16[64,80,256]{2,1,0:T(8,128)(2,1)}, u32[]{:S(2)}, u32[]{:S(2)}) async-start(bf16[64,80,256]{2,1,0:T(8,128)(2,1)} %bitcast.29), calls=%async_computation.1 | async-start | bytes 5242880 | tf_op jit(solution)/shard_map/all_to_all | solution.py:847
  90.8 4.1 %collective-permute-start.2 = (bf16[3072,256]{1,0:T(8,128)(2,1)}, bf16[3072,256]{1,0:T(8,128)(2,1)}, u32[]{:S(2)}, u32[]{:S(2)}) collective-permute-start(bf16[3072,256]{1,0:T(8,128)(2,1)} %get-tuple-element.88), channel_id=1, source_target_pairs={{0,1},{1,0},{2,3},{3,2},{4,5},{5,4},{6,7},{7,6},{8,9},{9,8},{10,11... | collective-permute-start | bytes 4718600 | tf_op jit(solution)/shard_map/ppermute | solution.py:761
  99.8 63.3 %all-to-all-start.2 = ((bf16[64,128,256]{2,1,0:T(8,128)(2,1)}), bf16[64,128,256]{2,1,0:T(8,128)(2,1)}, u32[]{:S(2)}, u32[]{:S(2)}) async-start(bf16[64,128,256]{2,1,0:T(8,128)(2,1)} %late_merge.1), calls=%async_computation.2 | async-start | bytes 8388608 | tf_op jit(solution)/shard_map/all_to_all | solution.py:887
  111.3 35.6 %collective-permute-start.5 = (bf16[256,256]{1,0:T(8,128)(2,1)S(1)}, bf16[256,256]{1,0:T(8,128)(2,1)S(1)}, u32[]{:S(2)}, u32[]{:S(2)}) collective-permute-start(bf16[256,256]{1,0:T(8,128)(2,1)S(1)} %get-tuple-element.121), channel_id=1, source_target_pairs={{0,96},{32,0},{64,32},{96,64},{1,97},{33,1},{65,33},{97,65},{2,98}... | collective-permute-start | bytes 393224 | tf_op jit(solution)/shard_map/ppermute | solution.py:894
  113.7 33.2 %collective-permute-start.4 = (bf16[256,256]{1,0:T(8,128)(2,1)S(1)}, bf16[256,256]{1,0:T(8,128)(2,1)S(1)}, u32[]{:S(2)}, u32[]{:S(2)}) collective-permute-start(bf16[256,256]{1,0:T(8,128)(2,1)S(1)} %get-tuple-element.122), channel_id=1, source_target_pairs={{0,64},{32,96},{64,0},{96,32},{1,65},{33,97},{65,1},{97,33},{2,66}... | collective-permute-start | bytes 393224 | tf_op jit(solution)/shard_map/ppermute | solution.py:894
  114.1 47.2 %collective-permute-start.3 = (bf16[256,256]{1,0:T(8,128)(2,1)S(1)}, bf16[256,256]{1,0:T(8,128)(2,1)S(1)}, u32[]{:S(2)}, u32[]{:S(2)}) collective-permute-start(bf16[256,256]{1,0:T(8,128)(2,1)S(1)} %get-tuple-element.123), channel_id=1, source_target_pairs={{0,32},{32,64},{64,96},{96,0},{1,33},{33,65},{65,97},{97,1},{2,34}... | collective-permute-start | bytes 393224 | tf_op jit(solution)/shard_map/ppermute | solution.py:894
  161.3 0.7 copy-start.1
  163.1 15.6 %collective-permute-start.6 = (bf16[64,128,256]{2,1,0:T(8,128)(2,1)}, bf16[64,128,256]{2,1,0:T(8,128)(2,1)}, u32[]{:S(2)}, u32[]{:S(2)}) collective-permute-start(bf16[64,128,256]{2,1,0:T(8,128)(2,1)} %all-to-all-done.2.parts_ref.mine_ref), channel_id=1, source_target_pairs={{0,1},{1,0},{2,3},{3,2},{4,5},{5,4},{6,7},{7,6},{8,9},{9,8},{10,11... | collective-permute-start | bytes 12582920 | tf_op jit(solution)/shard_map/ppermute | solution.py:761
  168.2 9.5 %copy-start.2 = (bf16[256,256]{1,0:T(8,128)(2,1)S(1)}, bf16[256,256]{1,0:T(8,128)(2,1)}, u32[]{:S(2)}) copy-start(bf16[256,256]{1,0:T(8,128)(2,1)} %copy-done.1) | copy-start | bytes 393220
  168.2 32.2 %all-to-all-start.3 = ((bf16[64,48,256]{2,1,0:T(8,128)(2,1)}), bf16[64,48,256]{2,1,0:T(8,128)(2,1)}, u32[]{:S(2)}, u32[]{:S(2)}) async-start(bf16[64,48,256]{2,1,0:T(8,128)(2,1)} %late_spread.1), calls=%async_computation.3 | async-start | bytes 3145728 | tf_op jit(solution)/shard_map/all_to_all | solution.py:911
  200.4 5.0 %collective-permute-start.7 = (bf16[3072,256]{1,0:T(8,128)(2,1)}, bf16[3072,256]{1,0:T(8,128)(2,1)S(1)}, u32[]{:S(2)}, u32[]{:S(2)}) collective-permute-start(bf16[3072,256]{1,0:T(8,128)(2,1)} %bitcast.19.rows_ref), channel_id=1, source_target_pairs={{0,1},{1,0},{2,3},{3,2},{4,5},{5,4},{6,7},{7,6},{8,9},{9,8},{10,11... | collective-permute-start | bytes 4718600 | tf_op jit(solution)/shard_map/ppermute | solution.py:761
where the time goes:
time: 212 us; the launch traced here: 209 us
  Pallas kernels  87.8 us (41%)
  waiting for transfers between devices  68.8 us (32%)
  starting transfers between devices  44.9 us (21%)
  local copies, waits for them, and re-layouts  3.28 us (2%)
  between operations  2.59 us (1%)
    pallas_call x11, Pallas kernels, call(): pl.pallas_call(kernel, grid_spec=pltpu.PrefetchScalarGridSpec(num_scalar_...  87.8 us
    ppermute x3, waiting for transfers between devices, body(): lax.ppermute(chunk, 'frame', [(i, (i + shift) % frame_count) for i in ran...  46.6 us
    all_to_all x1, waiting for transfers between devices, body(): lax.all_to_all(late_own, ring, split_axis=0, concat_axis=0, tiled=True)  14 us
    all_to_all x1, starting transfers between devices, body(): mixed = lax.all_to_all(mixed, ring, split_axis=0, concat_axis=0, tiled=True)  10.3 us
    all_to_all x1, starting transfers between devices, body(): lax.all_to_all(late_own, ring, split_axis=0, concat_axis=0, tiled=True)  8.78 us
    all_to_all x1, starting transfers between devices, body(): lax.all_to_all(early_sum.reshape(devices, -1, width), ring, split_axis=0,...  8.51 us
    ppermute x5, starting transfers between devices, swap_cores(): return lax.ppermute(array, 'core', [(0, 1), (1, 0)])  7.9 us
    ppermute x5, waiting for transfers between devices, swap_cores(): return lax.ppermute(array, 'core', [(0, 1), (1, 0)])  6.42 us
  transfers between devices with their start and end apart: 12, of which 7 were waited for; matrix products, arithmetic and copies ran while one was open for 2% of the time, Pallas kernels for 24%

commit v1 on v0

--- a/solution.py
+++ b/solution.py
@@ -18,7 +18,7 @@
 GELU_A = math.sqrt(2.0 / math.pi)
 GELU_B = GELU_A * 0.044715
 SMALL = 32
-FEED_CHUNK = 1024
+FEED_CHUNK = 512
 SPILL = 64
 
 
@@ -229,10 +229,10 @@
             lse_ref[pl.ds(2 * pair + odd, 1)] = highest + jnp.log(total)
 
     each_pair(attend)
+    between()
     context = ctx_t_ref[...].astype(F32).T.astype(BF)
     h1 = x_ref[...].astype(F32) + nn(context, out_ref[...]) + out_b_ref[0:1]
     h1_ref[...] = h1
-    between()
     unit, _ = normalise(h1)
     norm_b = (unit * gain_ref[1:2] + shift_ref[1:2]).astype(BF)
 
@@ -249,7 +249,7 @@
     y1_ref, norm_d_ref, cross_q_ref, cross_ref, mem_ref, cot_ref, gain_ref, shift_ref,
     in2_ref, out2_ref, out_b_ref, w1_ref, b1_ref, w2_ref, b2_ref,
     dec_ref, dmem_ref, early_ref, grad_ref, small_ref,
-    probs, turned, cross_t, dkv, dq_t,
+    probs, turned, cross_t, dkv, dq_t, fed,
 ):
     text, width = y1_ref.shape
     hidden_size = w1_ref.shape[1]
@@ -300,6 +300,7 @@
 
     zeros = jnp.zeros((text, width), F32)
     feed_out, grad_norm = lax.fori_loop(0, hidden_size // chunk, feed, (zeros, zeros))
+    fed()
     y3 = y2 + b2_ref[1:2] + feed_out
     dec_ref[...] = jnp.where(valid, y3, 0.0).astype(BF)
     small_ref[4:5] = col_sum(grad)
@@ -398,71 +399,105 @@
 
 def forward_and_decoder(
     tok_ref, len_ref, at_ref, core_ref,
-    x_ref, emb_ref, y1_ref, norm_c_ref, dec_qkv_ref, dec_ctx_t_ref, prob_ref, norm_d_ref, cross_q_ref,
-    cot_ref, gain_ref, shift_ref, in_ref, in_b_ref, out_ref, out_b_ref, w1_from, b1_ref, w2_from, b2_ref,
-    qkv_to, ctx_t_to, h1_to, lse_ref, dec_ref, dmem_ref, late_ref, swap_ref, keep_ref, send_ref,
-    value_t, act, mem, cross, probs, cross_t, dkv, dq_t, grad, small, early, sems,
-    w1_ref, w2_ref, qkv_ref, ctx_t_ref, h1_ref, load_sems, store_sems,
-):
-    loads = fetch(load_sems, (w1_from, w1_ref), (w2_from, w2_ref))
+    x_ref, in0, gain_ref, shift_ref, in_b_ref, out_b_ref, b1_ref, b2_ref,
+    in_from, out_from, w1_from, w2_from,
+    emb_from, y1_from, norm_c_from, dec_qkv_from, dec_ctx_t_from, prob_from, norm_d_from, cross_q_from, cot_from,
+    qkv_to, ctx_t_to, h1_to, lse_ref, dec_ref, dmem_to, late_ref, swap_ref, keep_ref, send_ref,
+    value_t, act, mem, cross, probs, cross_t, dkv, dq_t, grad, small, early,
+    qkv_ref, ctx_t_ref, h1_ref, dmem_ref,
+    in_ref, out_ref, w1_ref, w2_ref,
+    emb_ref, y1_ref, norm_c_ref, dec_qkv_ref, dec_ctx_t_ref, prob_ref, norm_d_ref, cross_q_ref, cot_ref,
+    load_sems, store_sems,
+):
+    loads = fetch(
+        load_sems, (out_from, out_ref), (w1_from, w1_ref), (w2_from, w2_ref), (in_from.at[1:], in_ref),
+        (emb_from, emb_ref), (y1_from, y1_ref), (norm_c_from, norm_c_ref), (dec_qkv_from, dec_qkv_ref),
+        (dec_ctx_t_from, dec_ctx_t_ref), (prob_from, prob_ref), (norm_d_from, norm_d_ref),
+        (cross_q_from, cross_q_ref), (cot_from, cot_ref),
+    )
     stores = []
 
-    def between():
-        stores.extend(fetch(store_sems, (qkv_ref, qkv_to), (ctx_t_ref, ctx_t_to), (h1_ref, h1_to)))
+    def send(*pairs):
+        for held, ref in pairs:
+            stores.append(pltpu.make_async_copy(held, ref, store_sems.at[len(stores)]))
+            stores[-1].start()
+
+    def arrived():
         for load in loads:
             load.wait()
-
-    in0, in1, in2 = (in_ref.at[i] for i in range(3))
+        send((qkv_ref, qkv_to), (ctx_t_ref, ctx_t_to))
+
+    in1, in2 = in_ref.at[0], in_ref.at[1]
     out0, out1, out2 = (out_ref.at[i] for i in range(3))
     encoder_forward(
         len_ref, at_ref, x_ref, gain_ref, shift_ref, in0, in_b_ref, out0, out_b_ref,
         w1_ref.at[0], b1_ref, w2_ref.at[0], b2_ref, in2,
         qkv_ref, ctx_t_ref, lse_ref, h1_ref, mem, cross,
-        value_t, act, between,
-    )
+        value_t, act, arrived,
+    )
+    half = early.shape[1]
+    full = half - 4 * x_ref.shape[1]
+    places = (keep_ref, send_ref)
+
+    def fed():
+        send((h1_ref, h1_to), *[(early.at[i, :full], places[i].at[:full]) for i in range(2)])
+
     decoder_main(
         tok_ref, len_ref, at_ref, core_ref,
         y1_ref, norm_d_ref, cross_q_ref, cross, mem, cot_ref, gain_ref, shift_ref,
         in2, out2, out_b_ref, w1_ref.at[1], b1_ref, w2_ref.at[1], b2_ref,
         dec_ref, dmem_ref, early, grad, small,
-        probs, value_t, cross_t, dkv, dq_t,
-    )
+        probs, value_t, cross_t, dkv, dq_t, fed,
+    )
+    send((dmem_ref, dmem_to), *[(early.at[i, full:], places[i].at[full:half]) for i in range(2)])
     decoder_self_backward(
         emb_ref, norm_c_ref, dec_qkv_ref, dec_ctx_t_ref, prob_ref, grad, small, gain_ref, in1, out1,
         late_ref, swap_ref,
     )
-    half = early.shape[1]
-    hand_out(
-        sems, (early.at[0], keep_ref), (early.at[1], send_ref.at[:half]), (swap_ref, send_ref.at[half:])
-    )
+    send((swap_ref, send_ref.at[half:]))
     for store in stores:
         store.wait()
 
 
 def encoder_backward(
     len_ref, at_ref, core_ref,
-    x_from, h1_ref, dmem_ref, ctx_t_ref, qkv_from, lse_ref, late_ref, gain_ref, shift_ref,
-    in_from, out_ref, w1_ref, b1_ref, w2_ref,
+    h1_ref, dmem_ref, lse_ref, gain_ref, shift_ref, w1_ref, b1_ref, w2_ref,
+    x_from, ctx_t_from, qkv_from, late_from, in_from, out_from,
     dx_ref, keep_ref, send_ref,
-    grad_hid, dh1, dctx, key_t, dq_t, dqkv, small, feed, attn, sems,
-    x_ref, qkv_ref, in_ref, load_sems, store_sems,
-):
-    loads = fetch(load_sems, (qkv_from, qkv_ref), (x_from, x_ref), (in_from.at[0], in_ref))
+    grad_hid, dh1, dctx, key_t, dq_t, dqkv, small, feed, attn,
+    x_ref, ctx_t_ref, qkv_ref, late_ref, in_ref, out_ref, load_sems, store_sems,
+):
+    loads = fetch(
+        load_sems, (ctx_t_from, ctx_t_ref), (late_from, late_ref), (out_from.at[0], out_ref),
+        (qkv_from, qkv_ref), (x_from, x_ref), (in_from.at[0], in_ref),
+    )
+    hidden = w1_ref.shape[1]
+    places = (keep_ref, send_ref)
+    stores = []
+
+    def send(*pairs):
+        for held, ref in pairs:
+            stores.append(pltpu.make_async_copy(held, ref, store_sems.at[len(stores)]))
+            stores[-1].start()
+
+    def fed():
+        for load in loads:
+            load.wait()
+        send(*[(feed.at[i, :hidden], places[i].at[:hidden]) for i in range(2)])
+
     encoder_feed_backward(
         core_ref, h1_ref, dmem_ref, ctx_t_ref, gain_ref, shift_ref, w1_ref, b1_ref, w2_ref, out_ref, late_ref,
         dh1, dctx, feed, small,
-        grad_hid,
+        grad_hid, fed,
     )
     cut = feed.shape[1]
-    stores = fetch(store_sems, (feed.at[0], keep_ref.at[:cut]), (feed.at[1], send_ref.at[:cut]))
-    for load in loads:
-        load.wait()
     encoder_attention_backward(
         len_ref, at_ref, core_ref, x_ref, qkv_ref, lse_ref, dctx, dh1, gain_ref, shift_ref, in_ref,
         dx_ref, attn,
         key_t, dq_t, dqkv, small,
     )
-    hand_out(sems, (attn.at[0], keep_ref.at[cut:]), (attn.at[1], send_ref.at[cut:]))
+    send(*[(feed.at[i, hidden:], places[i].at[hidden:cut]) for i in range(2)])
+    send(*[(attn.at[i], places[i].at[cut:]) for i in range(2)])
     for store in stores:
         store.wait()
 
@@ -552,32 +587,40 @@
         store.wait()
 
 
-def early_outputs(core_ref, rate_ref, mine_ref, other_ref, table_ref, in_ref, out_ref, w1_ref, w2_ref, rest_ref):
+def early_outputs(
+    core_ref, rate_ref, mine_ref, other_ref,
+    table_ref, in_ref, out_ref, w1_ref, w2_ref, rest_ref,
+    grads, table, sems,
+):
     rate = rate_ref[0]
     first = core_ref[0] == 0
     count, size, width = mine_ref.shape
-    blocks = w1_ref.shape[1] // width
-    half = in_ref.shape[0] * 2 + w2_ref.shape[0]
-    skip = size - 2 * half // count
-
-    def rows(core, part):
-        at = slice(count // 2 * part, count // 2 * (part + 1))
-        mine, other = mine_ref[at, skip:], other_ref[at, skip:]
-        picked = jnp.where(first, mine, other) if core == 0 else jnp.where(first, other, mine)
-        return picked.reshape(half, width)
-
-    table_ref[:half] = rows(0, 1).astype(F32) * rate
-    rest = rows(1, 1)
-    table_ref[half:] = rest[: table_ref.shape[0] - half].astype(F32) * rate
-    rest_ref[...] = rest[half - rest_ref.shape[0] :]
-    grads = jnp.concatenate([rows(0, 0), rows(1, 0)], axis=0).astype(F32) * rate
-    for block in range(blocks):
-        w1_ref[:, width * block : width * block + width] = grads[width * block : width * block + width]
-    w2_ref[...] = grads[width * blocks : 2 * width * blocks]
-    base = 2 * width * blocks
-    for part in range(3):
-        in_ref[:, width * part : width * part + width] = grads[base + width * part : base + width * part + width]
-    out_ref[...] = grads[base + 3 * width :]
+    hidden = w2_ref.shape[1]
+    half = grads.shape[0] // 2
+    each = 2 * half // count
+    skip = size - each
+
+    def chunk(index, carry):
+        at = pl.multiple_of(index * each, each)
+        for part, held in ((0, grads), (count // 2, table)):
+            mine, other = mine_ref[part + index, skip:], other_ref[part + index, skip:]
+            held[pl.ds(at, each)] = jnp.where(first, mine, other).astype(F32) * rate
+            held[pl.ds(half + at, each)] = jnp.where(first, other, mine).astype(F32) * rate
+        return carry
+
+    lax.fori_loop(0, count // 2, chunk, 0)
+    tail = mine_ref[count - 2 :, skip:].reshape(2 * each, width)
+    other_tail = other_ref[count - 2 :, skip:].reshape(2 * each, width)
+    rest_ref[...] = jnp.where(first, other_tail, tail)[2 * each - rest_ref.shape[0] :]
+    base = 2 * hidden
+    pairs = [(table.at[: table_ref.shape[0]], table_ref), (grads.at[hidden:base], w2_ref.at[1])]
+    pairs += [(grads.at[at : at + width], w1_ref.at[1, :, at : at + width]) for at in range(0, hidden, width)]
+    pairs += [
+        (grads.at[base + at : base + at + width], in_ref.at[2, :, at : at + width])
+        for at in range(0, 3 * width, width)
+    ]
+    pairs.append((grads.at[base + 3 * width :], out_ref.at[2]))
+    hand_out(sems, *pairs)
 
 
 def late_outputs(
@@ -593,7 +636,13 @@
     over = size - attn - width
     (load,) = fetch(sems, (rows_ref, rows))
     load.wait()
-    grads[:size] = rows[...].astype(F32) * rate_ref[0]
+
+    def scale(index, carry):
+        part = pl.ds(pl.multiple_of(index * width, width), width)
+        grads[part] = rows[part].astype(F32) * rate_ref[0]
+        return carry
+
+    lax.fori_loop(0, size // width, scale, 0)
     grads[size:] = early_ref[SMALL:].astype(F32) * rate_ref[0]
     rest_ref[...] = rows[size - 2 * SMALL : size - SMALL]
 
@@ -659,16 +708,12 @@
 def encoder_feed_backward(
     core_ref, h1_ref, dmem_ref, ctx_t_ref, gain_ref, shift_ref, w1_ref, b1_ref, w2_ref, out_ref, late_ref,
     dh1_ref, dctx_ref, feed_ref, small_ref,
-    grad_hid,
+    grad_hid, fed,
 ):
     width = h1_ref.shape[1]
     hidden_size = w1_ref.shape[1]
     slot = (core_ref[0], 1 - core_ref[0])
     cut = (width - SPILL) // 2
-    feed_ref[slot[0], hidden_size : hidden_size + 2 * width] = late_ref[: 2 * width]
-    feed_ref[slot[1], hidden_size : hidden_size + width] = late_ref[2 * width : 3 * width]
-    feed_ref[slot[0], hidden_size + 2 * width :] = late_ref[3 * width : 3 * width + cut]
-    feed_ref[slot[1], hidden_size + 2 * width :] = late_ref[3 * width + cut :]
     small_ref[...] = jnp.zeros_like(small_ref)
     unit, _ = normalise(h1_ref[...])
     norm_b = unit * gain_ref[1:2] + shift_ref[1:2]
@@ -695,6 +740,11 @@
         return carry
 
     lax.fori_loop(0, hidden_size // chunk, feed, 0)
+    fed()
+    feed_ref[slot[0], hidden_size : hidden_size + 2 * width] = late_ref[: 2 * width]
+    feed_ref[slot[1], hidden_size : hidden_size + width] = late_ref[2 * width : 3 * width]
+    feed_ref[slot[0], hidden_size + 2 * width :] = late_ref[3 * width : 3 * width + cut]
+    feed_ref[slot[1], hidden_size + 2 * width :] = late_ref[3 * width + cut :]
     grad = grad_low.astype(F32)
     small_ref[10:11] = col_sum(grad)
     unit, scale = normalise(h1_ref[...])
@@ -803,18 +853,19 @@
     )
     half = 2 * width + hidden
     swap_rows = text + SMALL + SPILL
+    decoder_args = [rows_in, y1, norm_c, dec_qkv, dec_ctx_t, dec_prob, norm_d, cross_q, cotangent[0, 0]]
     enc_qkv, enc_ctx_t, h1, lse, dec_out, dmem, self_grads, swap, early, early_send = call(
         forward_and_decoder,
         [
             ((rows, 3 * width), BF, None), ((width, rows), BF, None), ((rows, width), F32, None),
-            ((8, rows), F32), ((text, width), BF), ((rows, width), BF), ((4 * width - SPILL, width), BF),
+            ((8, rows), F32), ((text, width), BF), ((rows, width), BF, None), ((4 * width - SPILL, width), BF),
             ((swap_rows, width), BF), ((half, width), BF, None), ((half + swap_rows, width), BF, None),
         ],
         [
-            source, rows_in, y1, norm_c, dec_qkv, dec_ctx_t, dec_prob, norm_d, cross_q, cotangent[0, 0],
-            norm_gain, norm_bias, attn_in, attn_in_bias, attn_out, attn_out_bias, (ff_in, None), ff_in_bias,
-            (ff_out, None), ff_out_bias,
-        ],
+            source, (attn_in, 0), norm_gain, norm_bias, attn_in_bias, attn_out_bias, ff_in_bias, ff_out_bias,
+            (attn_in, None), (attn_out, None), (ff_in, None), (ff_out, None),
+        ]
+        + [(arg, None) for arg in decoder_args],
         [my_tok, lengths, frame_of, core_of],
         [
             pltpu.VMEM((width, rows), BF), pltpu.VMEM((rows, hidden), BF), pltpu.VMEM((rows, width), BF),
@@ -822,11 +873,13 @@
             pltpu.VMEM((width, text), F32), pltpu.VMEM((rows, 2 * width), BF),
             pltpu.VMEM((width, text), F32), pltpu.VMEM((text, width), F32),
             pltpu.VMEM((SMALL, width), F32), pltpu.VMEM((2, half, width), BF),
-            pltpu.SemaphoreType.DMA((3,)),
-            pltpu.VMEM(ff_in.shape, BF), pltpu.VMEM(ff_out.shape, BF), pltpu.VMEM((rows, 3 * width), BF),
-            pltpu.VMEM((width, rows), BF), pltpu.VMEM((rows, width), F32),
-            pltpu.SemaphoreType.DMA((2,)), pltpu.SemaphoreType.DMA((3,)),
-        ],
+            pltpu.VMEM((rows, 3 * width), BF), pltpu.VMEM((width, rows), BF), pltpu.VMEM((rows, width), F32),
+            pltpu.VMEM((rows, width), BF),
+            pltpu.VMEM((2,) + attn_in.shape[1:], BF), pltpu.VMEM(attn_out.shape, BF),
+            pltpu.VMEM(ff_in.shape, BF), pltpu.VMEM(ff_out.shape, BF),
+        ]
+        + [pltpu.VMEM(arg.shape, arg.dtype) for arg in decoder_args]
+        + [pltpu.SemaphoreType.DMA((13,)), pltpu.SemaphoreType.DMA((9,))],
         flops=2 * rows * width * (10 * width + 2 * rows + 2 * hidden)
         + 2 * text * width * (6 * hidden + 7 * rows + 26 * width),
     )
@@ -856,17 +909,18 @@
         encoder_backward,
         [((rows, width), BF), ((late_half, width), BF, None), ((late_half, width), BF, None)],
         [
-            (source, None), h1, dmem, enc_ctx_t, (enc_qkv, None), lse, self_grads, norm_gain, norm_bias,
-            (attn_in, None), (attn_out, 0), (ff_in, 0), ff_in_bias, (ff_out, 0),
+            h1, dmem, lse, norm_gain, norm_bias, (ff_in, 0), ff_in_bias, (ff_out, 0), (source, None),
+            (enc_ctx_t, None), (enc_qkv, None), (self_grads, None), (attn_in, None), (attn_out, None),
         ],
         [lengths, frame_of, core_of],
         [
             pltpu.VMEM((rows, hidden), BF), pltpu.VMEM((rows, width), F32), pltpu.VMEM((rows, width), BF),
             pltpu.VMEM((width, rows), BF), pltpu.VMEM((width, rows), F32), pltpu.VMEM((rows, 3 * width), BF),
             pltpu.VMEM((SMALL, width), F32), pltpu.VMEM((2, feed_half, width), BF),
-            pltpu.VMEM((2, attn_half, width), BF), pltpu.SemaphoreType.DMA((2,)),
-            pltpu.VMEM((rows, width), BF), pltpu.VMEM((rows, 3 * width), BF), pltpu.VMEM((width, 3 * width), BF),
-            pltpu.SemaphoreType.DMA((3,)), pltpu.SemaphoreType.DMA((2,)),
+            pltpu.VMEM((2, attn_half, width), BF),
+            pltpu.VMEM((rows, width), BF), pltpu.VMEM((width, rows), BF), pltpu.VMEM((rows, 3 * width), BF),
+            pltpu.VMEM(self_grads.shape, BF), pltpu.VMEM((width, 3 * width), BF), pltpu.VMEM((width, width), BF),
+            pltpu.SemaphoreType.DMA((6,)), pltpu.SemaphoreType.DMA((6,)),
         ],
         flops=2 * rows * width * (5 * hidden + 5 * rows + 8 * width),
     )
@@ -916,11 +970,15 @@
     table_grad, in_grad, out_grad, w1_grad, w2_grad, early_rest = call(
         early_outputs,
         [
-            ((vocab, width), F32), (in_shape, F32, None, 2), (out_shape, F32, None, 2),
-            (w1_shape, F32, None, 1), (w2_shape, F32, None, 1), ((SMALL + SPILL, width), BF),
+            ((vocab, width), F32, None), (in_shape, F32, None), (out_shape, F32, None),
+            (w1_shape, F32, None), (w2_shape, F32, None), ((SMALL + SPILL, width), BF),
         ],
         [mixed, early_other],
         [core_of, rate],
+        [
+            pltpu.VMEM((2 * half, width), F32), pltpu.VMEM((2 * half, width), F32),
+            pltpu.SemaphoreType.DMA((14,)),
+        ],
         limit=40,
     )
     late_mine, early_rest, frames_grad = lax.optimization_barrier((late_mine, early_rest, frames_grad))

time: 212 us -> 209 us (0.986); the launches traced: 209 us -> 208 us
  transfers between devices with their start and end apart: 12 -> 12, of which waited for: 7 -> 7; matrix products, arithmetic and copies ran while one was open for 2% -> 2% of each run, Pallas kernels for 24% -> 25%
where the time goes in v1:
time: 209 us; the launch traced here: 208 us
  Pallas kernels  88.9 us (43%)
  waiting for transfers between devices  67.7 us (32%)
  starting transfers between devices  44.9 us (21%)
  local copies, waits for them, and re-layouts  3.28 us (2%)
  between operations  2.15 us (1%)
    pallas_call x11, Pallas kernels, call(): pl.pallas_call(kernel, grid_spec=pltpu.PrefetchScalarGridSpec(num_scalar_...  88.9 us
    ppermute x3, waiting for transfers between devices, body(): lax.ppermute(chunk, 'frame', [(i, (i + shift) % frame_count) for i in ran...  46.6 us
    all_to_all x1, waiting for transfers between devices, body(): lax.all_to_all(late_own, ring, split_axis=0, concat_axis=0, tiled=True)  13 us
    all_to_all x1, starting transfers between devices, body(): mixed = lax.all_to_all(mixed, ring, split_axis=0, concat_axis=0, tiled=True)  10.3 us
    all_to_all x1, starting transfers between devices, body(): lax.all_to_all(late_own, ring, split_axis=0, concat_axis=0, tiled=True)  8.78 us
    all_to_all x1, starting transfers between devices, body(): lax.all_to_all(early_sum.reshape(devices, -1, width), ring, split_axis=0,...  8.51 us
    ppermute x5, starting transfers between devices, swap_cores(): return lax.ppermute(array, 'core', [(0, 1), (1, 0)])  7.91 us
    ppermute x5, waiting for transfers between devices, swap_cores(): return lax.ppermute(array, 'core', [(0, 1), (1, 0)])  6.42 us
  transfers between devices with their start and end apart: 12, of which 7 were waited for; matrix products, arithmetic and copies ran while one was open for 2% of the time, Pallas kernels for 25%

profile of v1, /device:TPU:1, one launch (start us, length us, event | category | flops | bytes accessed | tf_op | source)
XLA Modules:
  0.0 208.3 jit_solution(1618611456724848670)
XLA Ops:
  0.6 0.0 copy-start
  0.7 6.0 %all-to-all-start = ((bf16[4,256,256]{2,1,0:T(8,128)(2,1)}), bf16[4,256,256]{2,1,0:T(8,128)(2,1)}, u32[]{:S(2)}, u32[]{:S(2)}) async-start(bf16[4,256,256]{2,1,0:T(8,128)(2,1)} %bitcast.31), calls=%async_computation | async-start | bytes 1048576 | tf_op jit(solution)/shard_map/all_to_all | solution.py:832
  6.7 1.0 collective-permute-start
  7.6 0.7 fusion
  8.9 0.0 copy-done
  8.9 1.5 gather_fusion
  10.4 0.0 collective-permute-done
  10.4 0.7 pad_add_fusion
  11.1 3.3 %decoder_start.1 = (f32[128,256]{1,0:T(8,128)}, bf16[128,256]{1,0:T(8,128)(2,1)}, bf16[128,768]{1,0:T(8,128)(2,1)}, bf16[256,128]{1,0:T(8,128)(2,1)}, f32[4,128,...) custom-call(s32[1]{0:T(128)} %bitcast.26.tok_ref, bf16[128,256]{1,0:T(8,128)(2,1)} %gather_fusion, ...), custom_call_target="tpu_custom_call" | custom-call | flops 83886080 | bytes 3689472 | tf_op jit(solution)/shard_map/decoder_start/pallas_call | solution.py:142
  14.4 0.7 all-to-all-done
  15.0 26.9 %forward_and_decoder.1 = (bf16[1024,768]{1,0:T(8,128)(2,1)}, bf16[256,1024]{1,0:T(8,128)(2,1)}, f32[1024,256]{1,0:T(8,128)}, f32[8,1024]{1,0:T(8,128)}, bf16[128...) custom-call(s32[1]{0:T(128)} %bitcast.27.tok_ref, ...), custom_call_target="tpu_custom_call" | custom-call | flops 6274678784 | bytes 15602688 | tf_op jit(solution)/shard_map/forward_and_decoder/pallas_call | solution.py:142
  42.0 2.3 %collective-permute-start.1 = (bf16[2784,256]{1,0:T(8,128)(2,1)}, bf16[2784,256]{1,0:T(8,128)(2,1)S(1)}, u32[]{:S(2)}, u32[]{:S(2)}) collective-permute-start(bf16[2784,256]{1,0:T(8,128)(2,1)} %get-tuple-element.80), channel_id=1, source_target_pairs={{0,1},{1,0},{2,3},{3,2},{4,5},{5,4},{6,7},{7,6},{8,9},{9,8},{10,11... | collective-permute-start | bytes 4276232 | tf_op jit(solution)/shard_map/ppermute | solution.py:811
  44.2 3.0 %collective-permute-done.1.other_ref = bf16[2784,256]{1,0:T(8,128)(2,1)S(1)} collective-permute-done((bf16[2784,256]{1,0:T(8,128)(2,1)}, bf16[2784,256]{1,0:T(8,128)(2,1)S(1)}, u32[]{:S(2)}, u32[]{:S(2)}) %collective-permute-start.1) | collective-permute-done | bytes 1425440 | tf_op jit(solution)/shard_map/ppermute | solution.py:811
  47.3 3.0 %early_merge.1 = bf16[5120,256]{1,0:T(8,128)(2,1)} custom-call(s32[1]{0:T(128)} %bitcast.3.core_ref.half_ref, s32[1,256]{1,0:T(1,128)S(1)} %bitcast.28, bf16[224,256]{1,0:T(8,128)(2,1)} %get-tuple-element.78.swap_from, bf16[2560,256]{1,0:T(8,128)(2,1)} %get-tuple-element.79.keep_ref, bf16[2784,256]{1,0:T(8,128)(2,1)S(1)} %collective-permute-done.1.other_ref), custom_call_target="tpu_custom_call" | custom-call | flops 335544320 | bytes 5473280 | tf_op jit(solution)/shard_map/early_merge/pallas_call | solution.py:142
  50.2 8.5 %all-to-all-start.1 = ((bf16[64,80,256]{2,1,0:T(8,128)(2,1)}), bf16[64,80,256]{2,1,0:T(8,128)(2,1)}, u32[]{:S(2)}, u32[]{:S(2)}) async-start(bf16[64,80,256]{2,1,0:T(8,128)(2,1)} %bitcast.29), calls=%async_computation.1 | async-start | bytes 5242880 | tf_op jit(solution)/shard_map/all_to_all | solution.py:900
  58.7 32.1 %encoder_backward.1 = (bf16[1024,256]{1,0:T(8,128)(2,1)}, bf16[3072,256]{1,0:T(8,128)(2,1)}, bf16[3072,256]{1,0:T(8,128)(2,1)}) custom-call(s32[4]{0:T(128)} %bitcast.37, s32[1]{0:T(128)} %bitcast.2.at_ref.place_ref, s32[1]{0:T(128)} %bitcast.3.core_ref.half_ref, f32[1024,256]{1,0:T(8,128)} %get-tuple-element.76.h1_ref, ...), custom_call_target="tpu_custom_call" | custom-call | flops 9126805504 | bytes 14182400 | tf_op jit(solution)/shard_map/encoder_backward/pallas_call | solution.py:142
  90.9 0.7 collective-permute-start.2
  91.6 3.4 %collective-permute-done.2.other_ref = bf16[3072,256]{1,0:T(8,128)(2,1)} collective-permute-done((bf16[3072,256]{1,0:T(8,128)(2,1)}, bf16[3072,256]{1,0:T(8,128)(2,1)}, u32[]{:S(2)}, u32[]{:S(2)}) %collective-permute-start.2) | collective-permute-done | bytes 1572896 | tf_op jit(solution)/shard_map/ppermute | solution.py:811
  94.9 0.0 all-to-all-done.1.early_ref
  94.9 4.9 %late_merge.1 = bf16[64,128,256]{2,1,0:T(8,128)(2,1)} custom-call(bf16[3072,256]{1,0:T(8,128)(2,1)} %get-tuple-element.87.keep_ref, bf16[3072,256]{1,0:T(8,128)(2,1)} %collective-permute-done.2.other_ref, bf16[64,80,256]{2,1,0:T(8,128)(2,1)} %all-to-all-done.1.early_ref), custom_call_target="tpu_custom_call" | custom-call | bytes 9961472 | tf_op jit(solution)/shard_map/late_merge/pallas_call | solution.py:142
  99.8 10.3 %all-to-all-start.2 = ((bf16[64,128,256]{2,1,0:T(8,128)(2,1)}), bf16[64,128,256]{2,1,0:T(8,128)(2,1)}, u32[]{:S(2)}, u32[]{:S(2)}) async-start(bf16[64,128,256]{2,1,0:T(8,128)(2,1)} %late_merge.1), calls=%async_computation.2 | async-start | bytes 8388608 | tf_op jit(solution)/shard_map/all_to_all | solution.py:941
  110.1 1.1 dynamic-slice_bitcast_fusion
  111.3 2.4 %collective-permute-start.5 = (bf16[256,256]{1,0:T(8,128)(2,1)S(1)}, bf16[256,256]{1,0:T(8,128)(2,1)S(1)}, u32[]{:S(2)}, u32[]{:S(2)}) collective-permute-start(bf16[256,256]{1,0:T(8,128)(2,1)S(1)} %get-tuple-element.121), channel_id=1, source_target_pairs={{0,96},{32,0},{64,32},{96,64},{1,97},{33,1},{65,33},{97,65},{2,98}... | collective-permute-start | bytes 393224 | tf_op jit(solution)/shard_map/ppermute | solution.py:948
  113.7 0.4 collective-permute-start.4
  114.1 0.7 collective-permute-start.3
  114.8 32.2 %collective-permute-done.5.third_ref = bf16[256,256]{1,0:T(8,128)(2,1)S(1)} collective-permute-done((bf16[256,256]{1,0:T(8,128)(2,1)S(1)}, bf16[256,256]{1,0:T(8,128)(2,1)S(1)}, u32[]{:S(2)}, u32[]{:S(2)}) %collective-permute-start.5) | collective-permute-done | bytes 131104 | tf_op jit(solution)/shard_map/ppermute | solution.py:948
  146.9 0.0 collective-permute-done.4.second_ref
  146.9 14.4 %collective-permute-done.3.next_ref = bf16[256,256]{1,0:T(8,128)(2,1)S(1)} collective-permute-done((bf16[256,256]{1,0:T(8,128)(2,1)S(1)}, bf16[256,256]{1,0:T(8,128)(2,1)S(1)}, u32[]{:S(2)}, u32[]{:S(2)}) %collective-permute-start.3) | collective-permute-done | bytes 131104 | tf_op jit(solution)/shard_map/ppermute | solution.py:948
  161.3 0.0 copy-start.1
  161.3 0.7 copy-done.1
  162.0 1.1 all-to-all-done.2.parts_ref.mine_ref
  163.1 2.4 %collective-permute-start.6 = (bf16[64,128,256]{2,1,0:T(8,128)(2,1)}, bf16[64,128,256]{2,1,0:T(8,128)(2,1)}, u32[]{:S(2)}, u32[]{:S(2)}) collective-permute-start(bf16[64,128,256]{2,1,0:T(8,128)(2,1)} %all-to-all-done.2.parts_ref.mine_ref), channel_id=1, source_target_pairs={{0,1},{1,0},{2,3},{3,2},{4,5},{5,4},{6,7},{7,6},{8,9},{9,8},{10,11... | collective-permute-start | bytes 12582920 | tf_op jit(solution)/shard_map/ppermute | solution.py:811
  165.5 2.7 %late_spread.1 = bf16[64,48,256]{2,1,0:T(8,128)(2,1)} custom-call(bf16[64,128,256]{2,1,0:T(8,128)(2,1)} %all-to-all-done.2.parts_ref.mine_ref), custom_call_target="tpu_custom_call" | custom-call | bytes 5767168 | tf_op jit(solution)/shard_map/late_spread/pallas_call | solution.py:142
  168.2 0.0 copy-start.2
  168.2 8.8 %all-to-all-start.3 = ((bf16[64,48,256]{2,1,0:T(8,128)(2,1)}), bf16[64,48,256]{2,1,0:T(8,128)(2,1)}, u32[]{:S(2)}, u32[]{:S(2)}) async-start(bf16[64,48,256]{2,1,0:T(8,128)(2,1)} %late_spread.1), calls=%async_computation.3 | async-start | bytes 3145728 | tf_op jit(solution)/shard_map/all_to_all | solution.py:965
  177.7 0.0 copy-done.2
  177.7 1.0 frames_back.1
  178.7 0.0 collective-permute-done.6.other_ref
  178.7 8.7 %early_outputs.1 = (f32[5000,256]{1,0:T(8,128)}, f32[3,256,768]{2,1,0:T(8,128)}, f32[3,256,256]{2,1,0:T(8,128)}, f32[2,256,2048]{2,1,0:T(8,128)}, f32[2,2048,256]{2,1,0:T(8,128)}, /*index=5*/bf16[96,256]{1,0:T(8,128)(2,1)S(1)}) custom-call(s32[1]{0:T(128)} %bitcast.3.core_ref.half_ref, f32[1]{0:T(128)S(6)} %mul.9.rate_ref, ...), custom_call_target="tpu_custom_call" | custom-call | bytes 25092096 | tf_op jit(solution)/shard_map/early_outputs/pallas_call | solution.py:142
  187.4 13.0 %all-to-all-done.3 = bf16[64,48,256]{2,1,0:T(8,128)(2,1)} async-done(((bf16[64,48,256]{2,1,0:T(8,128)(2,1)}), bf16[64,48,256]{2,1,0:T(8,128)(2,1)}, u32[]{:S(2)}, u32[]{:S(2)}) %all-to-all-start.3) | async-done | bytes 1572896 | tf_op jit(solution)/shard_map/all_to_all | solution.py:965
  200.4 1.6 collective-permute-start.7
  202.0 3.5 %late_outputs.2 = (f32[3,256,768]{2,1,0:T(8,128)}, f32[3,256,256]{2,1,0:T(8,128)}, f32[2,256,2048]{2,1,0:T(8,128)}, f32[2,2048,256]{2,1,0:T(8,128)}, bf16[32,256]{1,0:T(8,128)(2,1)S(1)}) custom-call(s32[1]{0:T(128)} %bitcast.3.core_ref.half_ref, f32[1]{0:T(128)S(6)} %mul.9.rate_ref, ...), custom_call_target="tpu_custom_call", output_to_operand_aliasing={{0}: (4, {}), {1}: (5, {}), {2}: (6, {}), {3}: (7, {})} | custom-call | bytes 24707072 | tf_op jit(solution)/shard_map/late_outputs/pallas_call | solution.py:142
  205.5 0.0 collective-permute-done.7.rows_ref
  205.5 2.2 %late_outputs.3 = (f32[3,256,768]{2,1,0:T(8,128)}, f32[3,256,256]{2,1,0:T(8,128)}, f32[2,256,2048]{2,1,0:T(8,128)}, f32[2,2048,256]{2,1,0:T(8,128)}, bf16[32,256]{1,0:T(8,128)(2,1)S(1)}) custom-call(s32[1]{0:T(128)S(6)} %sub.3.half_ref, f32[1]{0:T(128)S(6)} %mul.9.rate_ref, ...), custom_call_target="tpu_custom_call", output_to_operand_aliasing={{0}: (4, {}), {1}: (5, {}), {2}: (6, {}), {3}: (7, {})} | custom-call | bytes 24707072 | tf_op jit(solution)/shard_map/late_outputs/pallas_call | solution.py:142
  207.7 0.6 small_outputs.1
  (1 shorter events, 0.0 us)
Async XLA Ops:
  0.6 8.3 %copy-start = (bf16[5000,256]{1,0:T(8,128)(2,1)S(1)}, bf16[5000,256]{1,0:T(8,128)(2,1)}, u32[]{:S(2)}) copy-start(bf16[5000,256]{1,0:T(8,128)(2,1)} %param.22) | copy-start | bytes 7680004
  0.7 14.4 %all-to-all-start = ((bf16[4,256,256]{2,1,0:T(8,128)(2,1)}), bf16[4,256,256]{2,1,0:T(8,128)(2,1)}, u32[]{:S(2)}, u32[]{:S(2)}) async-start(bf16[4,256,256]{2,1,0:T(8,128)(2,1)} %bitcast.31), calls=%async_computation | async-start | bytes 1048576 | tf_op jit(solution)/shard_map/all_to_all | solution.py:832
  6.7 3.8 %collective-permute-start = (s32[128]{0:T(128)}, s32[128]{0:T(128)S(1)}, u32[]{:S(2)}, u32[]{:S(2)}) collective-permute-start(s32[128]{0:T(128)} %bitcast.33), channel_id=1, source_target_pairs={{0,1},{1,0},{2,3},{3,2},{4,5},{5,4},{6,7},{7,6},{8,9},{9,8},{10,11... | collective-permute-start | bytes 1544 | tf_op jit(solution)/shard_map/ppermute | solution.py:811
  42.0 5.3 %collective-permute-start.1 = (bf16[2784,256]{1,0:T(8,128)(2,1)}, bf16[2784,256]{1,0:T(8,128)(2,1)S(1)}, u32[]{:S(2)}, u32[]{:S(2)}) collective-permute-start(bf16[2784,256]{1,0:T(8,128)(2,1)} %get-tuple-element.80), channel_id=1, source_target_pairs={{0,1},{1,0},{2,3},{3,2},{4,5},{5,4},{6,7},{7,6},{8,9},{9,8},{10,11... | collective-permute-start | bytes 4276232 | tf_op jit(solution)/shard_map/ppermute | solution.py:811
  50.2 44.7 %all-to-all-start.1 = ((bf16[64,80,256]{2,1,0:T(8,128)(2,1)}), bf16[64,80,256]{2,1,0:T(8,128)(2,1)}, u32[]{:S(2)}, u32[]{:S(2)}) async-start(bf16[64,80,256]{2,1,0:T(8,128)(2,1)} %bitcast.29), calls=%async_computation.1 | async-start | bytes 5242880 | tf_op jit(solution)/shard_map/all_to_all | solution.py:900
  90.9 4.1 %collective-permute-start.2 = (bf16[3072,256]{1,0:T(8,128)(2,1)}, bf16[3072,256]{1,0:T(8,128)(2,1)}, u32[]{:S(2)}, u32[]{:S(2)}) collective-permute-start(bf16[3072,256]{1,0:T(8,128)(2,1)} %get-tuple-element.88), channel_id=1, source_target_pairs={{0,1},{1,0},{2,3},{3,2},{4,5},{5,4},{6,7},{7,6},{8,9},{9,8},{10,11... | collective-permute-start | bytes 4718600 | tf_op jit(solution)/shard_map/ppermute | solution.py:811
  99.8 63.3 %all-to-all-start.2 = ((bf16[64,128,256]{2,1,0:T(8,128)(2,1)}), bf16[64,128,256]{2,1,0:T(8,128)(2,1)}, u32[]{:S(2)}, u32[]{:S(2)}) async-start(bf16[64,128,256]{2,1,0:T(8,128)(2,1)} %late_merge.1), calls=%async_computation.2 | async-start | bytes 8388608 | tf_op jit(solution)/shard_map/all_to_all | solution.py:941
  111.3 35.6 %collective-permute-start.5 = (bf16[256,256]{1,0:T(8,128)(2,1)S(1)}, bf16[256,256]{1,0:T(8,128)(2,1)S(1)}, u32[]{:S(2)}, u32[]{:S(2)}) collective-permute-start(bf16[256,256]{1,0:T(8,128)(2,1)S(1)} %get-tuple-element.121), channel_id=1, source_target_pairs={{0,96},{32,0},{64,32},{96,64},{1,97},{33,1},{65,33},{97,65},{2,98}... | collective-permute-start | bytes 393224 | tf_op jit(solution)/shard_map/ppermute | solution.py:948
  113.7 33.2 %collective-permute-start.4 = (bf16[256,256]{1,0:T(8,128)(2,1)S(1)}, bf16[256,256]{1,0:T(8,128)(2,1)S(1)}, u32[]{:S(2)}, u32[]{:S(2)}) collective-permute-start(bf16[256,256]{1,0:T(8,128)(2,1)S(1)} %get-tuple-element.122), channel_id=1, source_target_pairs={{0,64},{32,96},{64,0},{96,32},{1,65},{33,97},{65,1},{97,33},{2,66}... | collective-permute-start | bytes 393224 | tf_op jit(solution)/shard_map/ppermute | solution.py:948
  114.1 47.2 %collective-permute-start.3 = (bf16[256,256]{1,0:T(8,128)(2,1)S(1)}, bf16[256,256]{1,0:T(8,128)(2,1)S(1)}, u32[]{:S(2)}, u32[]{:S(2)}) collective-permute-start(bf16[256,256]{1,0:T(8,128)(2,1)S(1)} %get-tuple-element.123), channel_id=1, source_target_pairs={{0,32},{32,64},{64,96},{96,0},{1,33},{33,65},{65,97},{97,1},{2,34}... | collective-permute-start | bytes 393224 | tf_op jit(solution)/shard_map/ppermute | solution.py:948
  161.3 0.7 copy-start.1
  163.1 15.6 %collective-permute-start.6 = (bf16[64,128,256]{2,1,0:T(8,128)(2,1)}, bf16[64,128,256]{2,1,0:T(8,128)(2,1)}, u32[]{:S(2)}, u32[]{:S(2)}) collective-permute-start(bf16[64,128,256]{2,1,0:T(8,128)(2,1)} %all-to-all-done.2.parts_ref.mine_ref), channel_id=1, source_target_pairs={{0,1},{1,0},{2,3},{3,2},{4,5},{5,4},{6,7},{7,6},{8,9},{9,8},{10,11... | collective-permute-start | bytes 12582920 | tf_op jit(solution)/shard_map/ppermute | solution.py:811
  168.2 9.5 %copy-start.2 = (bf16[256,256]{1,0:T(8,128)(2,1)S(1)}, bf16[256,256]{1,0:T(8,128)(2,1)}, u32[]{:S(2)}) copy-start(bf16[256,256]{1,0:T(8,128)(2,1)} %copy-done.1) | copy-start | bytes 393220
  168.2 32.2 %all-to-all-start.3 = ((bf16[64,48,256]{2,1,0:T(8,128)(2,1)}), bf16[64,48,256]{2,1,0:T(8,128)(2,1)}, u32[]{:S(2)}, u32[]{:S(2)}) async-start(bf16[64,48,256]{2,1,0:T(8,128)(2,1)} %late_spread.1), calls=%async_computation.3 | async-start | bytes 3145728 | tf_op jit(solution)/shard_map/all_to_all | solution.py:965
  200.4 5.1 %collective-permute-start.7 = (bf16[3072,256]{1,0:T(8,128)(2,1)}, bf16[3072,256]{1,0:T(8,128)(2,1)S(1)}, u32[]{:S(2)}, u32[]{:S(2)}) collective-permute-start(bf16[3072,256]{1,0:T(8,128)(2,1)} %bitcast.19.rows_ref), channel_id=1, source_target_pairs={{0,1},{1,0},{2,3},{3,2},{4,5},{5,4},{6,7},{7,6},{8,9},{9,8},{10,11... | collective-permute-start | bytes 4718600 | tf_op jit(solution)/shard_map/ppermute | solution.py:811

commit v2 on v1

--- a/solution.py
+++ b/solution.py
@@ -94,6 +94,10 @@
     lane = lax.broadcasted_iota(jnp.int32, pair.shape, 1)
     mine = (lane < HEAD_DIM) if head % 2 == 0 else (lane >= HEAD_DIM)
     return jnp.where(mine, pair, jnp.zeros_like(pair))
+
+
+def both_heads(pair):
+    return jnp.concatenate([own_lanes(pair, 0), own_lanes(pair, 1)], axis=0)
 
 
 def spare_lane(head):
@@ -258,15 +262,16 @@
     turned[...] = cross_ref[:, width:].astype(F32).T.astype(BF)
 
     def attend(at, pair):
-        keys = cross_ref[:, pl.ds(at, 128)]
-        queries = cross_q_ref[:, pl.ds(at, 128)] * jnp.asarray(HEAD_DIM**-0.5, BF)
+        queries = both_heads(cross_q_ref[:, pl.ds(at, 128)] * jnp.asarray(HEAD_DIM**-0.5, BF))
+        score = nt(cross_ref[:, pl.ds(at, 128)], queries)
+        frame = lax.broadcasted_iota(jnp.int32, score.shape, 0)
+        score = jnp.where(frame < len_ref[at_ref[0]], score, MASKED)
+        weight = jnp.exp(score - jnp.max(score, axis=0, keepdims=True))
+        prob = weight * (1.0 / jnp.sum(weight, axis=0, keepdims=True))
+        probs[pair] = prob
+        full = nn(turned[pl.ds(at, 128)], prob.astype(BF))
         for odd in range(2):
-            query = with_one(own_lanes(queries, odd), odd)
-            score = nt(with_mask(keys, odd, len_ref[at_ref[0]]), query)
-            weight = jnp.exp(score - jnp.max(score, axis=0, keepdims=True))
-            prob = weight * (1.0 / jnp.sum(weight, axis=0, keepdims=True))
-            probs[2 * pair + odd] = prob
-            cross_t[head_rows(at, odd)] = nn(turned[head_rows(at, odd)], prob.astype(BF))
+            cross_t[head_rows(at, odd)] = full[HEAD_DIM * odd : HEAD_DIM * odd + HEAD_DIM, text * odd : text * odd + text]
 
     each_pair(attend)
     context_t = cross_t[...]
@@ -316,22 +321,17 @@
     grad_ref[...] = grad_ctx.astype(F32)
 
     def attend_backward(at, pair):
-        queries = cross_q_ref[:, pl.ds(at, 128)] * jnp.asarray(HEAD_DIM**-0.5, BF)
-        values = cross_ref[:, pl.ds(width + at, 128)]
-        grads = grad_ref[:, pl.ds(at, 128)].astype(BF)
-        dkey = 0.0
-        dvalue = 0.0
+        queries = both_heads(cross_q_ref[:, pl.ds(at, 128)] * jnp.asarray(HEAD_DIM**-0.5, BF))
+        grads = both_heads(grad_ref[:, pl.ds(at, 128)].astype(BF))
+        prob = probs[pair]
+        dprob = nt(cross_ref[:, pl.ds(width + at, 128)], grads)
+        inner = jnp.sum(dprob * prob, axis=0, keepdims=True)
+        dscore = (prob * (dprob - inner)).astype(BF)
+        dkv[:, pl.ds(at, 128)] = nn(dscore, queries).astype(BF)
+        dkv[:, pl.ds(width + at, 128)] = nn(prob.astype(BF), grads).astype(BF)
+        full = nn(turned[pl.ds(at, 128)], dscore)
         for odd in range(2):
-            own_grad = own_lanes(grads, odd)
-            prob = probs[2 * pair + odd]
-            dprob = nt(values, own_grad)
-            inner = jnp.sum(dprob * prob, axis=0, keepdims=True)
-            dscore = (prob * (dprob - inner)).astype(BF)
-            dvalue = dvalue + nn(prob.astype(BF), own_grad)
-            dkey = dkey + nn(dscore, own_lanes(queries, odd))
-            dq_t[head_rows(at, odd)] = nn(turned[head_rows(at, odd)], dscore)
-        dkv[:, pl.ds(at, 128)] = dkey.astype(BF)
-        dkv[:, pl.ds(width + at, 128)] = dvalue.astype(BF)
+            dq_t[head_rows(at, odd)] = full[HEAD_DIM * odd : HEAD_DIM * odd + HEAD_DIM, text * odd : text * odd + text]
 
     each_pair(attend_backward)
     dq = (dq_t[...] * HEAD_DIM**-0.5).T.astype(BF)
@@ -869,7 +869,7 @@
         [my_tok, lengths, frame_of, core_of],
         [
             pltpu.VMEM((width, rows), BF), pltpu.VMEM((rows, hidden), BF), pltpu.VMEM((rows, width), BF),
-            pltpu.VMEM((rows, 2 * width), BF), pltpu.VMEM((HEADS, rows, text), F32),
+            pltpu.VMEM((rows, 2 * width), BF), pltpu.VMEM((HEADS // 2, rows, 2 * text), F32),
             pltpu.VMEM((width, text), F32), pltpu.VMEM((rows, 2 * width), BF),
             pltpu.VMEM((width, text), F32), pltpu.VMEM((text, width), F32),
             pltpu.VMEM((SMALL, width), F32), pltpu.VMEM((2, half, width), BF),

time: 209 us -> 208 us (level)
  no operation moved by 1% of the time
where the time goes in v2:
time: 208 us; the launch traced here: 207 us
  Pallas kernels  87.8 us (42%)
  waiting for transfers between devices  67.7 us (33%)
  starting transfers between devices  45.2 us (22%)
  local copies, waits for them, and re-layouts  3.28 us (2%)
  between operations  2.15 us (1%)
    pallas_call x11, Pallas kernels, call(): pl.pallas_call(kernel, grid_spec=pltpu.PrefetchScalarGridSpec(num_scalar_...  87.8 us
    ppermute x3, waiting for transfers between devices, body(): lax.ppermute(chunk, 'frame', [(i, (i + shift) % frame_count) for i in ran...  46.6 us
    all_to_all x1, waiting for transfers between devices, body(): lax.all_to_all(late_own, ring, split_axis=0, concat_axis=0, tiled=True)  13 us
    all_to_all x1, starting transfers between devices, body(): mixed = lax.all_to_all(mixed, ring, split_axis=0, concat_axis=0, tiled=True)  10.3 us
    all_to_all x1, starting transfers between devices, body(): lax.all_to_all(late_own, ring, split_axis=0, concat_axis=0, tiled=True)  8.78 us
    all_to_all x1, starting transfers between devices, body(): lax.all_to_all(early_sum.reshape(devices, -1, width), ring, split_axis=0,...  8.51 us
    ppermute x5, starting transfers between devices, swap_cores(): return lax.ppermute(array, 'core', [(0, 1), (1, 0)])  8.12 us
    ppermute x5, waiting for transfers between devices, swap_cores(): return lax.ppermute(array, 'core', [(0, 1), (1, 0)])  6.42 us
  transfers between devices with their start and end apart: 12, of which 7 were waited for; matrix products, arithmetic and copies ran while one was open for 2% of the time, Pallas kernels for 25%

profile of v2, /device:TPU:1, one launch (start us, length us, event | category | flops | bytes accessed | tf_op | source)
XLA Modules:
  0.0 207.4 jit_solution(1749660229085319380)
XLA Ops:
  0.6 0.0 copy-start
  0.7 6.0 %all-to-all-start = ((bf16[4,256,256]{2,1,0:T(8,128)(2,1)}), bf16[4,256,256]{2,1,0:T(8,128)(2,1)}, u32[]{:S(2)}, u32[]{:S(2)}) async-start(bf16[4,256,256]{2,1,0:T(8,128)(2,1)} %bitcast.31), calls=%async_computation | async-start | bytes 1048576 | tf_op jit(solution)/shard_map/all_to_all | solution.py:832
  6.7 1.0 collective-permute-start
  7.6 0.7 fusion
  8.9 0.0 copy-done
  8.9 1.5 gather_fusion
  10.4 0.0 collective-permute-done
  10.4 0.7 pad_add_fusion
  11.1 3.3 %decoder_start.1 = (f32[128,256]{1,0:T(8,128)}, bf16[128,256]{1,0:T(8,128)(2,1)}, bf16[128,768]{1,0:T(8,128)(2,1)}, bf16[256,128]{1,0:T(8,128)(2,1)}, f32[4,128,...) custom-call(s32[1]{0:T(128)} %bitcast.26.tok_ref, bf16[128,256]{1,0:T(8,128)(2,1)} %gather_fusion, ...), custom_call_target="tpu_custom_call" | custom-call | flops 83886080 | bytes 3689472 | tf_op jit(solution)/shard_map/decoder_start/pallas_call | solution.py:146
  14.4 0.7 all-to-all-done
  15.0 25.8 %forward_and_decoder.1 = (bf16[1024,768]{1,0:T(8,128)(2,1)}, bf16[256,1024]{1,0:T(8,128)(2,1)}, f32[1024,256]{1,0:T(8,128)}, f32[8,1024]{1,0:T(8,128)}, bf16[128...) custom-call(s32[1]{0:T(128)} %bitcast.27.tok_ref, ...), custom_call_target="tpu_custom_call" | custom-call | flops 6274678784 | bytes 15602688 | tf_op jit(solution)/shard_map/forward_and_decoder/pallas_call | solution.py:146
  40.9 2.5 %collective-permute-start.1 = (bf16[2784,256]{1,0:T(8,128)(2,1)}, bf16[2784,256]{1,0:T(8,128)(2,1)S(1)}, u32[]{:S(2)}, u32[]{:S(2)}) collective-permute-start(bf16[2784,256]{1,0:T(8,128)(2,1)} %get-tuple-element.80), channel_id=1, source_target_pairs={{0,1},{1,0},{2,3},{3,2},{4,5},{5,4},{6,7},{7,6},{8,9},{9,8},{10,11... | collective-permute-start | bytes 4276232 | tf_op jit(solution)/shard_map/ppermute | solution.py:811
  43.3 3.0 %collective-permute-done.1.other_ref = bf16[2784,256]{1,0:T(8,128)(2,1)S(1)} collective-permute-done((bf16[2784,256]{1,0:T(8,128)(2,1)}, bf16[2784,256]{1,0:T(8,128)(2,1)S(1)}, u32[]{:S(2)}, u32[]{:S(2)}) %collective-permute-start.1) | collective-permute-done | bytes 1425440 | tf_op jit(solution)/shard_map/ppermute | solution.py:811
  46.3 3.0 %early_merge.1 = bf16[5120,256]{1,0:T(8,128)(2,1)} custom-call(s32[1]{0:T(128)} %bitcast.3.core_ref.half_ref, s32[1,256]{1,0:T(1,128)S(1)} %bitcast.28, bf16[224,256]{1,0:T(8,128)(2,1)} %get-tuple-element.78.swap_from, bf16[2560,256]{1,0:T(8,128)(2,1)} %get-tuple-element.79.keep_ref, bf16[2784,256]{1,0:T(8,128)(2,1)S(1)} %collective-permute-done.1.other_ref), custom_call_target="tpu_custom_call" | custom-call | flops 335544320 | bytes 5473280 | tf_op jit(solution)/shard_map/early_merge/pallas_call | solution.py:146
  49.3 8.5 %all-to-all-start.1 = ((bf16[64,80,256]{2,1,0:T(8,128)(2,1)}), bf16[64,80,256]{2,1,0:T(8,128)(2,1)}, u32[]{:S(2)}, u32[]{:S(2)}) async-start(bf16[64,80,256]{2,1,0:T(8,128)(2,1)} %bitcast.29), calls=%async_computation.1 | async-start | bytes 5242880 | tf_op jit(solution)/shard_map/all_to_all | solution.py:900
  57.8 32.1 %encoder_backward.1 = (bf16[1024,256]{1,0:T(8,128)(2,1)}, bf16[3072,256]{1,0:T(8,128)(2,1)}, bf16[3072,256]{1,0:T(8,128)(2,1)}) custom-call(s32[4]{0:T(128)} %bitcast.37, s32[1]{0:T(128)} %bitcast.2.at_ref.place_ref, s32[1]{0:T(128)} %bitcast.3.core_ref.half_ref, f32[1024,256]{1,0:T(8,128)} %get-tuple-element.76.h1_ref, ...), custom_call_target="tpu_custom_call" | custom-call | flops 9126805504 | bytes 14182400 | tf_op jit(solution)/shard_map/encoder_backward/pallas_call | solution.py:146
  89.9 0.7 collective-permute-start.2
  90.7 3.4 %collective-permute-done.2.other_ref = bf16[3072,256]{1,0:T(8,128)(2,1)} collective-permute-done((bf16[3072,256]{1,0:T(8,128)(2,1)}, bf16[3072,256]{1,0:T(8,128)(2,1)}, u32[]{:S(2)}, u32[]{:S(2)}) %collective-permute-start.2) | collective-permute-done | bytes 1572896 | tf_op jit(solution)/shard_map/ppermute | solution.py:811
  94.0 0.0 all-to-all-done.1.early_ref
  94.0 4.9 %late_merge.1 = bf16[64,128,256]{2,1,0:T(8,128)(2,1)} custom-call(bf16[3072,256]{1,0:T(8,128)(2,1)} %get-tuple-element.87.keep_ref, bf16[3072,256]{1,0:T(8,128)(2,1)} %collective-permute-done.2.other_ref, bf16[64,80,256]{2,1,0:T(8,128)(2,1)} %all-to-all-done.1.early_ref), custom_call_target="tpu_custom_call" | custom-call | bytes 9961472 | tf_op jit(solution)/shard_map/late_merge/pallas_call | solution.py:146
  98.9 10.3 %all-to-all-start.2 = ((bf16[64,128,256]{2,1,0:T(8,128)(2,1)}), bf16[64,128,256]{2,1,0:T(8,128)(2,1)}, u32[]{:S(2)}, u32[]{:S(2)}) async-start(bf16[64,128,256]{2,1,0:T(8,128)(2,1)} %late_merge.1), calls=%async_computation.2 | async-start | bytes 8388608 | tf_op jit(solution)/shard_map/all_to_all | solution.py:941
  109.2 1.1 dynamic-slice_bitcast_fusion
  110.4 2.4 %collective-permute-start.5 = (bf16[256,256]{1,0:T(8,128)(2,1)S(1)}, bf16[256,256]{1,0:T(8,128)(2,1)S(1)}, u32[]{:S(2)}, u32[]{:S(2)}) collective-permute-start(bf16[256,256]{1,0:T(8,128)(2,1)S(1)} %get-tuple-element.121), channel_id=1, source_target_pairs={{0,96},{32,0},{64,32},{96,64},{1,97},{33,1},{65,33},{97,65},{2,98}... | collective-permute-start | bytes 393224 | tf_op jit(solution)/shard_map/ppermute | solution.py:948
  112.8 0.4 collective-permute-start.4
  113.2 0.7 collective-permute-start.3
  113.9 32.2 %collective-permute-done.5.third_ref = bf16[256,256]{1,0:T(8,128)(2,1)S(1)} collective-permute-done((bf16[256,256]{1,0:T(8,128)(2,1)S(1)}, bf16[256,256]{1,0:T(8,128)(2,1)S(1)}, u32[]{:S(2)}, u32[]{:S(2)}) %collective-permute-start.5) | collective-permute-done | bytes 131104 | tf_op jit(solution)/shard_map/ppermute | solution.py:948
  146.0 0.0 collective-permute-done.4.second_ref
  146.0 14.4 %collective-permute-done.3.next_ref = bf16[256,256]{1,0:T(8,128)(2,1)S(1)} collective-permute-done((bf16[256,256]{1,0:T(8,128)(2,1)S(1)}, bf16[256,256]{1,0:T(8,128)(2,1)S(1)}, u32[]{:S(2)}, u32[]{:S(2)}) %collective-permute-start.3) | collective-permute-done | bytes 131104 | tf_op jit(solution)/shard_map/ppermute | solution.py:948
  160.4 0.0 copy-start.1
  160.4 0.7 copy-done.1
  161.1 1.1 all-to-all-done.2.parts_ref.mine_ref
  162.2 2.4 %collective-permute-start.6 = (bf16[64,128,256]{2,1,0:T(8,128)(2,1)}, bf16[64,128,256]{2,1,0:T(8,128)(2,1)}, u32[]{:S(2)}, u32[]{:S(2)}) collective-permute-start(bf16[64,128,256]{2,1,0:T(8,128)(2,1)} %all-to-all-done.2.parts_ref.mine_ref), channel_id=1, source_target_pairs={{0,1},{1,0},{2,3},{3,2},{4,5},{5,4},{6,7},{7,6},{8,9},{9,8},{10,11... | collective-permute-start | bytes 12582920 | tf_op jit(solution)/shard_map/ppermute | solution.py:811
  164.6 2.7 %late_spread.1 = bf16[64,48,256]{2,1,0:T(8,128)(2,1)} custom-call(bf16[64,128,256]{2,1,0:T(8,128)(2,1)} %all-to-all-done.2.parts_ref.mine_ref), custom_call_target="tpu_custom_call" | custom-call | bytes 5767168 | tf_op jit(solution)/shard_map/late_spread/pallas_call | solution.py:146
  167.3 0.0 copy-start.2
  167.3 8.8 %all-to-all-start.3 = ((bf16[64,48,256]{2,1,0:T(8,128)(2,1)}), bf16[64,48,256]{2,1,0:T(8,128)(2,1)}, u32[]{:S(2)}, u32[]{:S(2)}) async-start(bf16[64,48,256]{2,1,0:T(8,128)(2,1)} %late_spread.1), calls=%async_computation.3 | async-start | bytes 3145728 | tf_op jit(solution)/shard_map/all_to_all | solution.py:965
  176.8 0.0 copy-done.2
  176.8 1.0 frames_back.1
  177.8 0.0 collective-permute-done.6.other_ref
  177.8 8.7 %early_outputs.1 = (f32[5000,256]{1,0:T(8,128)}, f32[3,256,768]{2,1,0:T(8,128)}, f32[3,256,256]{2,1,0:T(8,128)}, f32[2,256,2048]{2,1,0:T(8,128)}, f32[2,2048,256]{2,1,0:T(8,128)}, /*index=5*/bf16[96,256]{1,0:T(8,128)(2,1)S(1)}) custom-call(s32[1]{0:T(128)} %bitcast.3.core_ref.half_ref, f32[1]{0:T(128)S(6)} %mul.9.rate_ref, ...), custom_call_target="tpu_custom_call" | custom-call | bytes 25092096 | tf_op jit(solution)/shard_map/early_outputs/pallas_call | solution.py:146
  186.5 13.0 %all-to-all-done.3 = bf16[64,48,256]{2,1,0:T(8,128)(2,1)} async-done(((bf16[64,48,256]{2,1,0:T(8,128)(2,1)}), bf16[64,48,256]{2,1,0:T(8,128)(2,1)}, u32[]{:S(2)}, u32[]{:S(2)}) %all-to-all-start.3) | async-done | bytes 1572896 | tf_op jit(solution)/shard_map/all_to_all | solution.py:965
  199.5 1.6 collective-permute-start.7
  201.1 3.5 %late_outputs.2 = (f32[3,256,768]{2,1,0:T(8,128)}, f32[3,256,256]{2,1,0:T(8,128)}, f32[2,256,2048]{2,1,0:T(8,128)}, f32[2,2048,256]{2,1,0:T(8,128)}, bf16[32,256]{1,0:T(8,128)(2,1)S(1)}) custom-call(s32[1]{0:T(128)} %bitcast.3.core_ref.half_ref, f32[1]{0:T(128)S(6)} %mul.9.rate_ref, ...), custom_call_target="tpu_custom_call", output_to_operand_aliasing={{0}: (4, {}), {1}: (5, {}), {2}: (6, {}), {3}: (7, {})} | custom-call | bytes 24707072 | tf_op jit(solution)/shard_map/late_outputs/pallas_call | solution.py:146
  204.6 0.0 collective-permute-done.7.rows_ref
  204.6 2.2 %late_outputs.3 = (f32[3,256,768]{2,1,0:T(8,128)}, f32[3,256,256]{2,1,0:T(8,128)}, f32[2,256,2048]{2,1,0:T(8,128)}, f32[2,2048,256]{2,1,0:T(8,128)}, bf16[32,256]{1,0:T(8,128)(2,1)S(1)}) custom-call(s32[1]{0:T(128)S(6)} %sub.3.half_ref, f32[1]{0:T(128)S(6)} %mul.9.rate_ref, ...), custom_call_target="tpu_custom_call", output_to_operand_aliasing={{0}: (4, {}), {1}: (5, {}), {2}: (6, {}), {3}: (7, {})} | custom-call | bytes 24707072 | tf_op jit(solution)/shard_map/late_outputs/pallas_call | solution.py:146
  206.8 0.6 small_outputs.1
  (1 shorter events, 0.0 us)
Async XLA Ops:
  0.6 8.3 %copy-start = (bf16[5000,256]{1,0:T(8,128)(2,1)S(1)}, bf16[5000,256]{1,0:T(8,128)(2,1)}, u32[]{:S(2)}) copy-start(bf16[5000,256]{1,0:T(8,128)(2,1)} %param.22) | copy-start | bytes 7680004
  0.7 14.4 %all-to-all-start = ((bf16[4,256,256]{2,1,0:T(8,128)(2,1)}), bf16[4,256,256]{2,1,0:T(8,128)(2,1)}, u32[]{:S(2)}, u32[]{:S(2)}) async-start(bf16[4,256,256]{2,1,0:T(8,128)(2,1)} %bitcast.31), calls=%async_computation | async-start | bytes 1048576 | tf_op jit(solution)/shard_map/all_to_all | solution.py:832
  6.7 3.8 %collective-permute-start = (s32[128]{0:T(128)}, s32[128]{0:T(128)S(1)}, u32[]{:S(2)}, u32[]{:S(2)}) collective-permute-start(s32[128]{0:T(128)} %bitcast.33), channel_id=1, source_target_pairs={{0,1},{1,0},{2,3},{3,2},{4,5},{5,4},{6,7},{7,6},{8,9},{9,8},{10,11... | collective-permute-start | bytes 1544 | tf_op jit(solution)/shard_map/ppermute | solution.py:811
  40.9 5.5 %collective-permute-start.1 = (bf16[2784,256]{1,0:T(8,128)(2,1)}, bf16[2784,256]{1,0:T(8,128)(2,1)S(1)}, u32[]{:S(2)}, u32[]{:S(2)}) collective-permute-start(bf16[2784,256]{1,0:T(8,128)(2,1)} %get-tuple-element.80), channel_id=1, source_target_pairs={{0,1},{1,0},{2,3},{3,2},{4,5},{5,4},{6,7},{7,6},{8,9},{9,8},{10,11... | collective-permute-start | bytes 4276232 | tf_op jit(solution)/shard_map/ppermute | solution.py:811
  49.3 44.7 %all-to-all-start.1 = ((bf16[64,80,256]{2,1,0:T(8,128)(2,1)}), bf16[64,80,256]{2,1,0:T(8,128)(2,1)}, u32[]{:S(2)}, u32[]{:S(2)}) async-start(bf16[64,80,256]{2,1,0:T(8,128)(2,1)} %bitcast.29), calls=%async_computation.1 | async-start | bytes 5242880 | tf_op jit(solution)/shard_map/all_to_all | solution.py:900
  89.9 4.1 %collective-permute-start.2 = (bf16[3072,256]{1,0:T(8,128)(2,1)}, bf16[3072,256]{1,0:T(8,128)(2,1)}, u32[]{:S(2)}, u32[]{:S(2)}) collective-permute-start(bf16[3072,256]{1,0:T(8,128)(2,1)} %get-tuple-element.88), channel_id=1, source_target_pairs={{0,1},{1,0},{2,3},{3,2},{4,5},{5,4},{6,7},{7,6},{8,9},{9,8},{10,11... | collective-permute-start | bytes 4718600 | tf_op jit(solution)/shard_map/ppermute | solution.py:811
  98.9 63.3 %all-to-all-start.2 = ((bf16[64,128,256]{2,1,0:T(8,128)(2,1)}), bf16[64,128,256]{2,1,0:T(8,128)(2,1)}, u32[]{:S(2)}, u32[]{:S(2)}) async-start(bf16[64,128,256]{2,1,0:T(8,128)(2,1)} %late_merge.1), calls=%async_computation.2 | async-start | bytes 8388608 | tf_op jit(solution)/shard_map/all_to_all | solution.py:941
  110.4 35.6 %collective-permute-start.5 = (bf16[256,256]{1,0:T(8,128)(2,1)S(1)}, bf16[256,256]{1,0:T(8,128)(2,1)S(1)}, u32[]{:S(2)}, u32[]{:S(2)}) collective-permute-start(bf16[256,256]{1,0:T(8,128)(2,1)S(1)} %get-tuple-element.121), channel_id=1, source_target_pairs={{0,96},{32,0},{64,32},{96,64},{1,97},{33,1},{65,33},{97,65},{2,98}... | collective-permute-start | bytes 393224 | tf_op jit(solution)/shard_map/ppermute | solution.py:948
  112.8 33.2 %collective-permute-start.4 = (bf16[256,256]{1,0:T(8,128)(2,1)S(1)}, bf16[256,256]{1,0:T(8,128)(2,1)S(1)}, u32[]{:S(2)}, u32[]{:S(2)}) collective-permute-start(bf16[256,256]{1,0:T(8,128)(2,1)S(1)} %get-tuple-element.122), channel_id=1, source_target_pairs={{0,64},{32,96},{64,0},{96,32},{1,65},{33,97},{65,1},{97,33},{2,66}... | collective-permute-start | bytes 393224 | tf_op jit(solution)/shard_map/ppermute | solution.py:948
  113.2 47.2 %collective-permute-start.3 = (bf16[256,256]{1,0:T(8,128)(2,1)S(1)}, bf16[256,256]{1,0:T(8,128)(2,1)S(1)}, u32[]{:S(2)}, u32[]{:S(2)}) collective-permute-start(bf16[256,256]{1,0:T(8,128)(2,1)S(1)} %get-tuple-element.123), channel_id=1, source_target_pairs={{0,32},{32,64},{64,96},{96,0},{1,33},{33,65},{65,97},{97,1},{2,34}... | collective-permute-start | bytes 393224 | tf_op jit(solution)/shard_map/ppermute | solution.py:948
  160.4 0.7 copy-start.1
  162.2 15.6 %collective-permute-start.6 = (bf16[64,128,256]{2,1,0:T(8,128)(2,1)}, bf16[64,128,256]{2,1,0:T(8,128)(2,1)}, u32[]{:S(2)}, u32[]{:S(2)}) collective-permute-start(bf16[64,128,256]{2,1,0:T(8,128)(2,1)} %all-to-all-done.2.parts_ref.mine_ref), channel_id=1, source_target_pairs={{0,1},{1,0},{2,3},{3,2},{4,5},{5,4},{6,7},{7,6},{8,9},{9,8},{10,11... | collective-permute-start | bytes 12582920 | tf_op jit(solution)/shard_map/ppermute | solution.py:811
  167.3 9.5 %copy-start.2 = (bf16[256,256]{1,0:T(8,128)(2,1)S(1)}, bf16[256,256]{1,0:T(8,128)(2,1)}, u32[]{:S(2)}) copy-start(bf16[256,256]{1,0:T(8,128)(2,1)} %copy-done.1) | copy-start | bytes 393220
  167.3 32.2 %all-to-all-start.3 = ((bf16[64,48,256]{2,1,0:T(8,128)(2,1)}), bf16[64,48,256]{2,1,0:T(8,128)(2,1)}, u32[]{:S(2)}, u32[]{:S(2)}) async-start(bf16[64,48,256]{2,1,0:T(8,128)(2,1)} %late_spread.1), calls=%async_computation.3 | async-start | bytes 3145728 | tf_op jit(solution)/shard_map/all_to_all | solution.py:965
  199.5 5.1 %collective-permute-start.7 = (bf16[3072,256]{1,0:T(8,128)(2,1)}, bf16[3072,256]{1,0:T(8,128)(2,1)S(1)}, u32[]{:S(2)}, u32[]{:S(2)}) collective-permute-start(bf16[3072,256]{1,0:T(8,128)(2,1)} %bitcast.19.rows_ref), channel_id=1, source_target_pairs={{0,1},{1,0},{2,3},{3,2},{4,5},{5,4},{6,7},{7,6},{8,9},{9,8},{10,11... | collective-permute-start | bytes 4718600 | tf_op jit(solution)/shard_map/ppermute | solution.py:811

commit v3 on v2

--- a/solution.py
+++ b/solution.py
@@ -88,6 +88,37 @@
 
 def head_rows(at, odd):
     return pl.ds(pl.multiple_of(at + HEAD_DIM * odd, HEAD_DIM), HEAD_DIM)
+
+
+def spread_heads(rows):
+    lane = lax.broadcasted_iota(jnp.int32, rows.shape, 1)
+    zero = jnp.zeros_like(rows)
+    heads = range(0, HEADS * HEAD_DIM, HEAD_DIM)
+    own = [jnp.logical_and(lane >= at, lane < at + HEAD_DIM) for at in heads]
+    return jnp.concatenate([jnp.where(mine, rows, zero) for mine in own], axis=0)
+
+
+def own_blocks(full):
+    count = full.shape[1] // HEADS
+    return jnp.concatenate(
+        [full[HEAD_DIM * h : HEAD_DIM * (h + 1), count * h : count * (h + 1)] for h in range(HEADS)], axis=0
+    )
+
+
+def attend_all(keys, values_t, queries, seen):
+    score = jnp.where(seen, nt(keys, queries), MASKED)
+    weight = jnp.exp(score - jnp.max(score, axis=0, keepdims=True))
+    prob = weight * (1.0 / jnp.sum(weight, axis=0, keepdims=True))
+    return prob, own_blocks(nn(values_t, prob.astype(BF)))
+
+
+def attend_all_backward(keys_t, values, queries, grads, prob):
+    dprob = nt(values, grads)
+    inner = jnp.sum(dprob * prob, axis=0, keepdims=True)
+    dscore = (prob * (dprob - inner)).astype(BF)
+    dkeys = nn(dscore, queries).astype(BF)
+    dvalues = nn(prob.astype(BF), grads).astype(BF)
+    return dkeys, dvalues, own_blocks(nn(keys_t, dscore)) * HEAD_DIM**-0.5
 
 
 def own_lanes(pair, head):
@@ -180,20 +211,13 @@
     qkv_ref[:, width : 2 * width] = key
     qkv_ref[:, 2 * width :] = value
     value_t = value.astype(F32).T.astype(BF)
-    key_at = lax.broadcasted_iota(jnp.int32, (text, text), 0)
-    query_at = lax.broadcasted_iota(jnp.int32, (text, text), 1)
+    shape = (text, HEADS * text)
+    key_at = lax.broadcasted_iota(jnp.int32, shape, 0)
+    query_at = lax.rem(lax.broadcasted_iota(jnp.int32, shape, 1), text)
     seen = jnp.logical_and(key_at <= query_at, key_at < tok_ref[0])
-    scaled = query * jnp.asarray(HEAD_DIM**-0.5, BF)
-    parts = []
-    for head in range(HEADS):
-        lanes = lanes_of(head)
-        score = nt(key[:, lanes], own_lanes(scaled[:, lanes], head))
-        score = jnp.where(seen, score, MASKED)
-        weight = jnp.exp(score - jnp.max(score, axis=0, keepdims=True))
-        prob = weight / jnp.sum(weight, axis=0, keepdims=True)
-        prob_ref[head] = prob
-        parts.append(nn(value_t[rows_of(head)], prob.astype(BF)))
-    ctx_t = jnp.concatenate(parts, axis=0)
+    queries = spread_heads(query * jnp.asarray(HEAD_DIM**-0.5, BF))
+    prob, ctx_t = attend_all(key, value_t, queries, seen)
+    prob_ref[...] = prob
     ctx_t_ref[...] = ctx_t.astype(BF)
     y1 = start + nn(ctx_t.T.astype(BF), out_ref[...]) + out_b_ref[1:2]
     y1_ref[...] = y1
@@ -362,28 +386,12 @@
     late_ref[3 * width :] = dout1[: width - SPILL]
     swap_ref[text + SMALL :] = dout1[width - SPILL :]
     grad_ctx = nt(grad_low, out1_ref[...]).astype(BF)
-    key_t = qkv_ref[:, width : 2 * width].astype(F32).T.astype(BF)
-    scaled = qkv_ref[:, :width] * jnp.asarray(HEAD_DIM**-0.5, BF)
-    dkeys = []
-    dvalues = []
-    dquery = []
-    for pair in range(HEADS // 2):
-        dkey = 0.0
-        dvalue = 0.0
-        for head in (2 * pair, 2 * pair + 1):
-            lanes = lanes_of(head)
-            own_grad = own_lanes(grad_ctx[:, lanes], head)
-            prob = prob_ref[head]
-            dprob = nt(qkv_ref[:, slice(2 * width + lanes.start, 2 * width + lanes.stop)], own_grad)
-            inner = jnp.sum(dprob * prob, axis=0, keepdims=True)
-            dscore = (prob * (dprob - inner)).astype(BF)
-            dvalue = dvalue + nn(prob.astype(BF), own_grad)
-            dkey = dkey + nn(dscore, own_lanes(scaled[:, lanes], head))
-            dquery.append(nn(key_t[rows_of(head)], dscore))
-        dkeys.append(dkey.astype(BF))
-        dvalues.append(dvalue.astype(BF))
-    dq_t = jnp.concatenate(dquery, axis=0) * HEAD_DIM**-0.5
-    dqkv = jnp.concatenate([dq_t.T.astype(BF)] + dkeys + dvalues, axis=1)
+    keys_t = qkv_ref[:, width : 2 * width].astype(F32).T.astype(BF)
+    queries = spread_heads(qkv_ref[:, :width] * jnp.asarray(HEAD_DIM**-0.5, BF))
+    dkeys, dvalues, dq_t = attend_all_backward(
+        keys_t, qkv_ref[:, 2 * width :], queries, spread_heads(grad_ctx), prob_ref[...]
+    )
+    dqkv = jnp.concatenate([dq_t.T.astype(BF), dkeys, dvalues], axis=1)
     small_ref[11:12] = col_sum(dqkv[:, :width])
     small_ref[12:13] = col_sum(dqkv[:, 2 * width :])
     din1 = nn(norm_c_ref[...].astype(F32).T.astype(BF), dqkv).astype(BF)
@@ -842,7 +850,7 @@
         decoder_start,
         [
             ((text, width), F32), ((text, width), BF), ((text, 3 * width), BF), ((width, text), BF),
-            ((HEADS, text, text), F32), ((text, width), BF), ((text, width), BF),
+            ((text, HEADS * text), F32), ((text, width), BF), ((text, width), BF),
         ],
         [
             rows_in, norm_gain, norm_bias, (attn_in, 1), attn_in_bias, (attn_out, 1),

time: 208 us -> 208 us (level)
  no operation moved by 1% of the time
where the time goes in v3:
time: 208 us; the launch traced here: 207 us
  Pallas kernels  87.2 us (42%)
  waiting for transfers between devices  67.8 us (33%)
  starting transfers between devices  45.2 us (22%)
  local copies, waits for them, and re-layouts  3.28 us (2%)
  between operations  2.15 us (1%)
    pallas_call x11, Pallas kernels, call(): pl.pallas_call(kernel, grid_spec=pltpu.PrefetchScalarGridSpec(num_scalar_...  87.2 us
    ppermute x3, waiting for transfers between devices, body(): lax.ppermute(chunk, 'frame', [(i, (i + shift) % frame_count) for i in ran...  46.6 us
    all_to_all x1, waiting for transfers between devices, body(): lax.all_to_all(late_own, ring, split_axis=0, concat_axis=0, tiled=True)  13 us
    all_to_all x1, starting transfers between devices, body(): mixed = lax.all_to_all(mixed, ring, split_axis=0, concat_axis=0, tiled=True)  10.3 us
    all_to_all x1, starting transfers between devices, body(): lax.all_to_all(late_own, ring, split_axis=0, concat_axis=0, tiled=True)  8.78 us
    all_to_all x1, starting transfers between devices, body(): lax.all_to_all(early_sum.reshape(devices, -1, width), ring, split_axis=0,...  8.51 us
    ppermute x5, starting transfers between devices, swap_cores(): return lax.ppermute(array, 'core', [(0, 1), (1, 0)])  8.13 us
    ppermute x5, waiting for transfers between devices, swap_cores(): return lax.ppermute(array, 'core', [(0, 1), (1, 0)])  6.42 us
  transfers between devices with their start and end apart: 12, of which 7 were waited for; matrix products, arithmetic and copies ran while one was open for 2% of the time, Pallas kernels for 25%

profile of v3, /device:TPU:1, one launch (start us, length us, event | category | flops | bytes accessed | tf_op | source)
XLA Modules:
  0.0 206.9 jit_solution(15581735446453716763)
XLA Ops:
  0.6 0.0 copy-start
  0.7 6.0 %all-to-all-start = ((bf16[4,256,256]{2,1,0:T(8,128)(2,1)}), bf16[4,256,256]{2,1,0:T(8,128)(2,1)}, u32[]{:S(2)}, u32[]{:S(2)}) async-start(bf16[4,256,256]{2,1,0:T(8,128)(2,1)} %bitcast.31), calls=%async_computation | async-start | bytes 1048576 | tf_op jit(solution)/shard_map/all_to_all | solution.py:840
  6.7 1.0 collective-permute-start
  7.6 0.7 fusion
  8.9 0.0 copy-done
  8.9 1.5 gather_fusion
  10.4 0.0 collective-permute-done
  10.4 0.7 pad_add_fusion
  11.1 3.2 %decoder_start.1 = (f32[128,256]{1,0:T(8,128)}, bf16[128,256]{1,0:T(8,128)(2,1)}, bf16[128,768]{1,0:T(8,128)(2,1)}, bf16[256,128]{1,0:T(8,128)(2,1)}, f32[128,51...) custom-call(s32[1]{0:T(128)} %bitcast.26.tok_ref, bf16[128,256]{1,0:T(8,128)(2,1)} %gather_fusion, ...), custom_call_target="tpu_custom_call" | custom-call | flops 83886080 | bytes 3689472 | tf_op jit(solution)/shard_map/decoder_start/pallas_call | solution.py:177
  14.3 0.8 all-to-all-done
  15.0 25.3 %forward_and_decoder.1 = (bf16[1024,768]{1,0:T(8,128)(2,1)}, bf16[256,1024]{1,0:T(8,128)(2,1)}, f32[1024,256]{1,0:T(8,128)}, f32[8,1024]{1,0:T(8,128)}, bf16[128...) custom-call(s32[1]{0:T(128)} %bitcast.27.tok_ref, ...), custom_call_target="tpu_custom_call" | custom-call | flops 6274678784 | bytes 15602688 | tf_op jit(solution)/shard_map/forward_and_decoder/pallas_call | solution.py:177
  40.4 2.5 %collective-permute-start.1 = (bf16[2784,256]{1,0:T(8,128)(2,1)}, bf16[2784,256]{1,0:T(8,128)(2,1)S(1)}, u32[]{:S(2)}, u32[]{:S(2)}) collective-permute-start(bf16[2784,256]{1,0:T(8,128)(2,1)} %get-tuple-element.80), channel_id=1, source_target_pairs={{0,1},{1,0},{2,3},{3,2},{4,5},{5,4},{6,7},{7,6},{8,9},{9,8},{10,11... | collective-permute-start | bytes 4276232 | tf_op jit(solution)/shard_map/ppermute | solution.py:819
  42.8 3.0 %collective-permute-done.1.other_ref = bf16[2784,256]{1,0:T(8,128)(2,1)S(1)} collective-permute-done((bf16[2784,256]{1,0:T(8,128)(2,1)}, bf16[2784,256]{1,0:T(8,128)(2,1)S(1)}, u32[]{:S(2)}, u32[]{:S(2)}) %collective-permute-start.1) | collective-permute-done | bytes 1425440 | tf_op jit(solution)/shard_map/ppermute | solution.py:819
  45.9 3.0 %early_merge.1 = bf16[5120,256]{1,0:T(8,128)(2,1)} custom-call(s32[1]{0:T(128)} %bitcast.3.core_ref.half_ref, s32[1,256]{1,0:T(1,128)S(1)} %bitcast.28, bf16[224,256]{1,0:T(8,128)(2,1)} %get-tuple-element.78.swap_from, bf16[2560,256]{1,0:T(8,128)(2,1)} %get-tuple-element.79.keep_ref, bf16[2784,256]{1,0:T(8,128)(2,1)S(1)} %collective-permute-done.1.other_ref), custom_call_target="tpu_custom_call" | custom-call | flops 335544320 | bytes 5473280 | tf_op jit(solution)/shard_map/early_merge/pallas_call | solution.py:177
  48.8 8.5 %all-to-all-start.1 = ((bf16[64,80,256]{2,1,0:T(8,128)(2,1)}), bf16[64,80,256]{2,1,0:T(8,128)(2,1)}, u32[]{:S(2)}, u32[]{:S(2)}) async-start(bf16[64,80,256]{2,1,0:T(8,128)(2,1)} %bitcast.29), calls=%async_computation.1 | async-start | bytes 5242880 | tf_op jit(solution)/shard_map/all_to_all | solution.py:908
  57.4 32.1 %encoder_backward.1 = (bf16[1024,256]{1,0:T(8,128)(2,1)}, bf16[3072,256]{1,0:T(8,128)(2,1)}, bf16[3072,256]{1,0:T(8,128)(2,1)}) custom-call(s32[4]{0:T(128)} %bitcast.37, s32[1]{0:T(128)} %bitcast.2.at_ref.place_ref, s32[1]{0:T(128)} %bitcast.3.core_ref.half_ref, f32[1024,256]{1,0:T(8,128)} %get-tuple-element.76.h1_ref, ...), custom_call_target="tpu_custom_call" | custom-call | flops 9126805504 | bytes 14182400 | tf_op jit(solution)/shard_map/encoder_backward/pallas_call | solution.py:177
  89.5 0.7 collective-permute-start.2
  90.2 3.4 %collective-permute-done.2.other_ref = bf16[3072,256]{1,0:T(8,128)(2,1)} collective-permute-done((bf16[3072,256]{1,0:T(8,128)(2,1)}, bf16[3072,256]{1,0:T(8,128)(2,1)}, u32[]{:S(2)}, u32[]{:S(2)}) %collective-permute-start.2) | collective-permute-done | bytes 1572896 | tf_op jit(solution)/shard_map/ppermute | solution.py:819
  93.6 0.0 all-to-all-done.1.early_ref
  93.6 4.9 %late_merge.1 = bf16[64,128,256]{2,1,0:T(8,128)(2,1)} custom-call(bf16[3072,256]{1,0:T(8,128)(2,1)} %get-tuple-element.87.keep_ref, bf16[3072,256]{1,0:T(8,128)(2,1)} %collective-permute-done.2.other_ref, bf16[64,80,256]{2,1,0:T(8,128)(2,1)} %all-to-all-done.1.early_ref), custom_call_target="tpu_custom_call" | custom-call | bytes 9961472 | tf_op jit(solution)/shard_map/late_merge/pallas_call | solution.py:177
  98.5 10.3 %all-to-all-start.2 = ((bf16[64,128,256]{2,1,0:T(8,128)(2,1)}), bf16[64,128,256]{2,1,0:T(8,128)(2,1)}, u32[]{:S(2)}, u32[]{:S(2)}) async-start(bf16[64,128,256]{2,1,0:T(8,128)(2,1)} %late_merge.1), calls=%async_computation.2 | async-start | bytes 8388608 | tf_op jit(solution)/shard_map/all_to_all | solution.py:949
  108.8 1.1 dynamic-slice_bitcast_fusion
  109.9 2.4 %collective-permute-start.5 = (bf16[256,256]{1,0:T(8,128)(2,1)S(1)}, bf16[256,256]{1,0:T(8,128)(2,1)S(1)}, u32[]{:S(2)}, u32[]{:S(2)}) collective-permute-start(bf16[256,256]{1,0:T(8,128)(2,1)S(1)} %get-tuple-element.121), channel_id=1, source_target_pairs={{0,96},{32,0},{64,32},{96,64},{1,97},{33,1},{65,33},{97,65},{2,98}... | collective-permute-start | bytes 393224 | tf_op jit(solution)/shard_map/ppermute | solution.py:956
  112.3 0.4 collective-permute-start.4
  112.7 0.7 collective-permute-start.3
  113.4 32.2 %collective-permute-done.5.third_ref = bf16[256,256]{1,0:T(8,128)(2,1)S(1)} collective-permute-done((bf16[256,256]{1,0:T(8,128)(2,1)S(1)}, bf16[256,256]{1,0:T(8,128)(2,1)S(1)}, u32[]{:S(2)}, u32[]{:S(2)}) %collective-permute-start.5) | collective-permute-done | bytes 131104 | tf_op jit(solution)/shard_map/ppermute | solution.py:956
  145.5 0.0 collective-permute-done.4.second_ref
  145.5 14.4 %collective-permute-done.3.next_ref = bf16[256,256]{1,0:T(8,128)(2,1)S(1)} collective-permute-done((bf16[256,256]{1,0:T(8,128)(2,1)S(1)}, bf16[256,256]{1,0:T(8,128)(2,1)S(1)}, u32[]{:S(2)}, u32[]{:S(2)}) %collective-permute-start.3) | collective-permute-done | bytes 131104 | tf_op jit(solution)/shard_map/ppermute | solution.py:956
  160.0 0.0 copy-start.1
  160.0 0.7 copy-done.1
  160.6 1.1 all-to-all-done.2.parts_ref.mine_ref
  161.7 2.4 %collective-permute-start.6 = (bf16[64,128,256]{2,1,0:T(8,128)(2,1)}, bf16[64,128,256]{2,1,0:T(8,128)(2,1)}, u32[]{:S(2)}, u32[]{:S(2)}) collective-permute-start(bf16[64,128,256]{2,1,0:T(8,128)(2,1)} %all-to-all-done.2.parts_ref.mine_ref), channel_id=1, source_target_pairs={{0,1},{1,0},{2,3},{3,2},{4,5},{5,4},{6,7},{7,6},{8,9},{9,8},{10,11... | collective-permute-start | bytes 12582920 | tf_op jit(solution)/shard_map/ppermute | solution.py:819
  164.1 2.7 %late_spread.1 = bf16[64,48,256]{2,1,0:T(8,128)(2,1)} custom-call(bf16[64,128,256]{2,1,0:T(8,128)(2,1)} %all-to-all-done.2.parts_ref.mine_ref), custom_call_target="tpu_custom_call" | custom-call | bytes 5767168 | tf_op jit(solution)/shard_map/late_spread/pallas_call | solution.py:177
  166.8 0.0 copy-start.2
  166.8 8.8 %all-to-all-start.3 = ((bf16[64,48,256]{2,1,0:T(8,128)(2,1)}), bf16[64,48,256]{2,1,0:T(8,128)(2,1)}, u32[]{:S(2)}, u32[]{:S(2)}) async-start(bf16[64,48,256]{2,1,0:T(8,128)(2,1)} %late_spread.1), calls=%async_computation.3 | async-start | bytes 3145728 | tf_op jit(solution)/shard_map/all_to_all | solution.py:973
  176.3 0.0 copy-done.2
  176.3 1.0 frames_back.1
  177.4 0.0 collective-permute-done.6.other_ref
  177.4 8.7 %early_outputs.1 = (f32[5000,256]{1,0:T(8,128)}, f32[3,256,768]{2,1,0:T(8,128)}, f32[3,256,256]{2,1,0:T(8,128)}, f32[2,256,2048]{2,1,0:T(8,128)}, f32[2,2048,256]{2,1,0:T(8,128)}, /*index=5*/bf16[96,256]{1,0:T(8,128)(2,1)S(1)}) custom-call(s32[1]{0:T(128)} %bitcast.3.core_ref.half_ref, f32[1]{0:T(128)S(6)} %mul.9.rate_ref, ...), custom_call_target="tpu_custom_call" | custom-call | bytes 25092096 | tf_op jit(solution)/shard_map/early_outputs/pallas_call | solution.py:177
  186.0 13.0 %all-to-all-done.3 = bf16[64,48,256]{2,1,0:T(8,128)(2,1)} async-done(((bf16[64,48,256]{2,1,0:T(8,128)(2,1)}), bf16[64,48,256]{2,1,0:T(8,128)(2,1)}, u32[]{:S(2)}, u32[]{:S(2)}) %all-to-all-start.3) | async-done | bytes 1572896 | tf_op jit(solution)/shard_map/all_to_all | solution.py:973
  199.0 1.6 collective-permute-start.7
  200.6 3.5 %late_outputs.2 = (f32[3,256,768]{2,1,0:T(8,128)}, f32[3,256,256]{2,1,0:T(8,128)}, f32[2,256,2048]{2,1,0:T(8,128)}, f32[2,2048,256]{2,1,0:T(8,128)}, bf16[32,256]{1,0:T(8,128)(2,1)S(1)}) custom-call(s32[1]{0:T(128)} %bitcast.3.core_ref.half_ref, f32[1]{0:T(128)S(6)} %mul.9.rate_ref, ...), custom_call_target="tpu_custom_call", output_to_operand_aliasing={{0}: (4, {}), {1}: (5, {}), {2}: (6, {}), {3}: (7, {})} | custom-call | bytes 24707072 | tf_op jit(solution)/shard_map/late_outputs/pallas_call | solution.py:177
  204.1 0.0 collective-permute-done.7.rows_ref
  204.1 2.2 %late_outputs.3 = (f32[3,256,768]{2,1,0:T(8,128)}, f32[3,256,256]{2,1,0:T(8,128)}, f32[2,256,2048]{2,1,0:T(8,128)}, f32[2,2048,256]{2,1,0:T(8,128)}, bf16[32,256]{1,0:T(8,128)(2,1)S(1)}) custom-call(s32[1]{0:T(128)S(6)} %sub.3.half_ref, f32[1]{0:T(128)S(6)} %mul.9.rate_ref, ...), custom_call_target="tpu_custom_call", output_to_operand_aliasing={{0}: (4, {}), {1}: (5, {}), {2}: (6, {}), {3}: (7, {})} | custom-call | bytes 24707072 | tf_op jit(solution)/shard_map/late_outputs/pallas_call | solution.py:177
  206.3 0.6 small_outputs.1
  (1 shorter events, 0.0 us)
Async XLA Ops:
  0.6 8.3 %copy-start = (bf16[5000,256]{1,0:T(8,128)(2,1)S(1)}, bf16[5000,256]{1,0:T(8,128)(2,1)}, u32[]{:S(2)}) copy-start(bf16[5000,256]{1,0:T(8,128)(2,1)} %param.22) | copy-start | bytes 7680004
  0.7 14.4 %all-to-all-start = ((bf16[4,256,256]{2,1,0:T(8,128)(2,1)}), bf16[4,256,256]{2,1,0:T(8,128)(2,1)}, u32[]{:S(2)}, u32[]{:S(2)}) async-start(bf16[4,256,256]{2,1,0:T(8,128)(2,1)} %bitcast.31), calls=%async_computation | async-start | bytes 1048576 | tf_op jit(solution)/shard_map/all_to_all | solution.py:840
  6.7 3.8 %collective-permute-start = (s32[128]{0:T(128)}, s32[128]{0:T(128)S(1)}, u32[]{:S(2)}, u32[]{:S(2)}) collective-permute-start(s32[128]{0:T(128)} %bitcast.33), channel_id=1, source_target_pairs={{0,1},{1,0},{2,3},{3,2},{4,5},{5,4},{6,7},{7,6},{8,9},{9,8},{10,11... | collective-permute-start | bytes 1544 | tf_op jit(solution)/shard_map/ppermute | solution.py:819
  40.4 5.5 %collective-permute-start.1 = (bf16[2784,256]{1,0:T(8,128)(2,1)}, bf16[2784,256]{1,0:T(8,128)(2,1)S(1)}, u32[]{:S(2)}, u32[]{:S(2)}) collective-permute-start(bf16[2784,256]{1,0:T(8,128)(2,1)} %get-tuple-element.80), channel_id=1, source_target_pairs={{0,1},{1,0},{2,3},{3,2},{4,5},{5,4},{6,7},{7,6},{8,9},{9,8},{10,11... | collective-permute-start | bytes 4276232 | tf_op jit(solution)/shard_map/ppermute | solution.py:819
  48.8 44.7 %all-to-all-start.1 = ((bf16[64,80,256]{2,1,0:T(8,128)(2,1)}), bf16[64,80,256]{2,1,0:T(8,128)(2,1)}, u32[]{:S(2)}, u32[]{:S(2)}) async-start(bf16[64,80,256]{2,1,0:T(8,128)(2,1)} %bitcast.29), calls=%async_computation.1 | async-start | bytes 5242880 | tf_op jit(solution)/shard_map/all_to_all | solution.py:908
  89.5 4.1 %collective-permute-start.2 = (bf16[3072,256]{1,0:T(8,128)(2,1)}, bf16[3072,256]{1,0:T(8,128)(2,1)}, u32[]{:S(2)}, u32[]{:S(2)}) collective-permute-start(bf16[3072,256]{1,0:T(8,128)(2,1)} %get-tuple-element.88), channel_id=1, source_target_pairs={{0,1},{1,0},{2,3},{3,2},{4,5},{5,4},{6,7},{7,6},{8,9},{9,8},{10,11... | collective-permute-start | bytes 4718600 | tf_op jit(solution)/shard_map/ppermute | solution.py:819
  98.5 63.3 %all-to-all-start.2 = ((bf16[64,128,256]{2,1,0:T(8,128)(2,1)}), bf16[64,128,256]{2,1,0:T(8,128)(2,1)}, u32[]{:S(2)}, u32[]{:S(2)}) async-start(bf16[64,128,256]{2,1,0:T(8,128)(2,1)} %late_merge.1), calls=%async_computation.2 | async-start | bytes 8388608 | tf_op jit(solution)/shard_map/all_to_all | solution.py:949
  109.9 35.6 %collective-permute-start.5 = (bf16[256,256]{1,0:T(8,128)(2,1)S(1)}, bf16[256,256]{1,0:T(8,128)(2,1)S(1)}, u32[]{:S(2)}, u32[]{:S(2)}) collective-permute-start(bf16[256,256]{1,0:T(8,128)(2,1)S(1)} %get-tuple-element.121), channel_id=1, source_target_pairs={{0,96},{32,0},{64,32},{96,64},{1,97},{33,1},{65,33},{97,65},{2,98}... | collective-permute-start | bytes 393224 | tf_op jit(solution)/shard_map/ppermute | solution.py:956
  112.3 33.2 %collective-permute-start.4 = (bf16[256,256]{1,0:T(8,128)(2,1)S(1)}, bf16[256,256]{1,0:T(8,128)(2,1)S(1)}, u32[]{:S(2)}, u32[]{:S(2)}) collective-permute-start(bf16[256,256]{1,0:T(8,128)(2,1)S(1)} %get-tuple-element.122), channel_id=1, source_target_pairs={{0,64},{32,96},{64,0},{96,32},{1,65},{33,97},{65,1},{97,33},{2,66}... | collective-permute-start | bytes 393224 | tf_op jit(solution)/shard_map/ppermute | solution.py:956
  112.7 47.2 %collective-permute-start.3 = (bf16[256,256]{1,0:T(8,128)(2,1)S(1)}, bf16[256,256]{1,0:T(8,128)(2,1)S(1)}, u32[]{:S(2)}, u32[]{:S(2)}) collective-permute-start(bf16[256,256]{1,0:T(8,128)(2,1)S(1)} %get-tuple-element.123), channel_id=1, source_target_pairs={{0,32},{32,64},{64,96},{96,0},{1,33},{33,65},{65,97},{97,1},{2,34}... | collective-permute-start | bytes 393224 | tf_op jit(solution)/shard_map/ppermute | solution.py:956
  160.0 0.7 copy-start.1
  161.7 15.6 %collective-permute-start.6 = (bf16[64,128,256]{2,1,0:T(8,128)(2,1)}, bf16[64,128,256]{2,1,0:T(8,128)(2,1)}, u32[]{:S(2)}, u32[]{:S(2)}) collective-permute-start(bf16[64,128,256]{2,1,0:T(8,128)(2,1)} %all-to-all-done.2.parts_ref.mine_ref), channel_id=1, source_target_pairs={{0,1},{1,0},{2,3},{3,2},{4,5},{5,4},{6,7},{7,6},{8,9},{9,8},{10,11... | collective-permute-start | bytes 12582920 | tf_op jit(solution)/shard_map/ppermute | solution.py:819
  166.8 9.5 %copy-start.2 = (bf16[256,256]{1,0:T(8,128)(2,1)S(1)}, bf16[256,256]{1,0:T(8,128)(2,1)}, u32[]{:S(2)}) copy-start(bf16[256,256]{1,0:T(8,128)(2,1)} %copy-done.1) | copy-start | bytes 393220
  166.8 32.2 %all-to-all-start.3 = ((bf16[64,48,256]{2,1,0:T(8,128)(2,1)}), bf16[64,48,256]{2,1,0:T(8,128)(2,1)}, u32[]{:S(2)}, u32[]{:S(2)}) async-start(bf16[64,48,256]{2,1,0:T(8,128)(2,1)} %late_spread.1), calls=%async_computation.3 | async-start | bytes 3145728 | tf_op jit(solution)/shard_map/all_to_all | solution.py:973
  199.0 5.1 %collective-permute-start.7 = (bf16[3072,256]{1,0:T(8,128)(2,1)}, bf16[3072,256]{1,0:T(8,128)(2,1)S(1)}, u32[]{:S(2)}, u32[]{:S(2)}) collective-permute-start(bf16[3072,256]{1,0:T(8,128)(2,1)} %bitcast.19.rows_ref), channel_id=1, source_target_pairs={{0,1},{1,0},{2,3},{3,2},{4,5},{5,4},{6,7},{7,6},{8,9},{9,8},{10,11... | collective-permute-start | bytes 4718600 | tf_op jit(solution)/shard_map/ppermute | solution.py:819
